TPU v7x, 128 devices: a whole 4x4x4 slice. The times are simulated.
128 devices in a mesh: grp: 4 (over y), dev: 32 (over x, z, core).
Axes of the slice: x: 4, y: 4, z: 4, core: 2. Of those that a mesh axis runs over, the one named last changes fastest.
Arguments:
- text: bfloat16 [32768, 2048], P(('grp', 'dev')), may hold values from -6 to 6
- targets: int32 [32768, 1], P(('grp', 'dev')), may hold values from 0 to 127; in each aligned block of 256 rows (0 to 255, 256 to 511, ...) at most 4 rows name the same one
- negatives: int32 [32768, 8], P(('grp', 'dev')), may hold values from 0 to 255
- row_weight: float32 [32768, 1], P(('grp', 'dev')), may hold values from 0.5 to 13.5
- boundary: int32 [128, 128], P(('grp', 'dev')), may hold values from 0 to 511
- tile_index: int32 [128, 4, 4], P(('grp', 'dev')), may hold values from 0 to 35
- adjacency: bfloat16 [128, 4, 4, 128, 128], P(('grp', 'dev')), may hold values from -0.25 to 0.25
- w_proj: bfloat16 [2048, 1024], replicated, may hold values from -0.125 to 0.125
- w_gnn: bfloat16 [1024, 1024], replicated, may hold values from -0.1875 to 0.1875
Outputs:
- loss: float32 [], replicated
- grad_proj: float32 [2048, 1024], replicated
- grad_gnn: float32 [1024, 1024], replicated
Inputs may be any that keep to these rules, and one draw needn't show every extreme that they name: `targets`: among the rows of one device at most 4 name the same owner, and in every draw some owner is named by exactly 4 of some device's rows. `tile_index`: values under 4 name the owner's own tiles; value 4 + d names the boundary rows of device d of the partition.
All inputs are finite; a program needn't handle non-finite values.
Results may differ from a plain program's by a relative error of at most 0.015.
Values may be sent and summed in bfloat16 or wider, within the bound.
No kernel may reach another device: no remote copies, remote signals or barrier semaphores. Data moves between devices by JAX's collectives and lax.ppermute only.
A program may use at most 128 MiB of HBM per device.

v0:
```python
import jax
import jax.numpy as jnp
from jax import lax
from jax.sharding import PartitionSpec as P

logit_scale = 8.0
logit_bias = -4.0


def placement_matrix(targets, owners, capacity):
    labels = jnp.arange(owners, dtype=jnp.int32)
    onehot = (targets[:, None] == labels[None, :]).astype(jnp.int32)
    earlier = jnp.cumsum(onehot, axis=0) - onehot
    ranking = jnp.sum(earlier * onehot, axis=1)
    position = targets * capacity + ranking
    columns = jnp.arange(owners * capacity, dtype=jnp.int32)
    return (columns[:, None] == position[None, :]).astype(jnp.bfloat16)


def contrast(graph_rows, text_rows, partners, weights):
    unit_graph = graph_rows * lax.rsqrt(
        jnp.sum(graph_rows * graph_rows, axis=1, keepdims=True) + 1e-06
    )
    unit_text = text_rows * lax.rsqrt(jnp.sum(text_rows * text_rows, axis=1, keepdims=True) + 1e-06)
    similar = jnp.dot(unit_graph, unit_text.T, precision=lax.Precision.HIGHEST)
    positive = jnp.sum(unit_graph * unit_text, axis=1)
    negative = jnp.take_along_axis(similar, partners, axis=1)
    per_row = jax.nn.softplus(-(logit_scale * positive + logit_bias)) + jnp.sum(
        jax.nn.softplus(logit_scale * negative + logit_bias), axis=1
    )
    return jnp.sum(weights[:, 0] * per_row)


def layer_forward(held, extra, tile_index, adjacency, w_gnn):
    tile_rows = adjacency.shape[-1]
    width = held.shape[1]
    sources = jnp.concatenate([held, extra], axis=0).reshape(-1, tile_rows, width)
    picked = sources[tile_index]
    summed = (
        jnp.einsum("bkij,bkjh->bih", adjacency, picked, preferred_element_type=jnp.float32)
        .reshape(held.shape)
        .astype(jnp.bfloat16)
    )
    before = jnp.dot(summed, w_gnn, preferred_element_type=jnp.float32)
    return (summed, before, jax.nn.silu(before).astype(jnp.bfloat16))


def layer_backward(summed, before, tile_index, adjacency, w_gnn, upstream, members):
    blocks = adjacency.shape[0]
    tile_rows = adjacency.shape[-1]
    width = summed.shape[1]
    sigma = jax.nn.sigmoid(before)
    slope = (upstream.astype(jnp.float32) * sigma * (1.0 + before * (1.0 - sigma))).astype(
        jnp.bfloat16
    )
    grad_gnn = jnp.einsum("sh,sg->hg", summed, slope, preferred_element_type=jnp.float32)
    grad_sum = jnp.einsum("sg,hg->sh", slope, w_gnn, preferred_element_type=jnp.float32).astype(
        jnp.bfloat16
    )
    term = jnp.einsum(
        "bkij,bih->bkjh",
        adjacency,
        grad_sum.reshape(blocks, tile_rows, width),
        preferred_element_type=jnp.float32,
    )
    selector = (
        tile_index[None, :, :] == jnp.arange(blocks + members, dtype=jnp.int32)[:, None, None]
    ).astype(jnp.float32)
    grad_tiles = jnp.einsum("tbk,bkjh->tjh", selector, term, precision=lax.Precision.HIGHEST)
    local = grad_tiles[:blocks].reshape(blocks * tile_rows, width)
    remote = grad_tiles[blocks:].reshape(members * tile_rows, width)
    return (grad_gnn, local, remote)


def body(text, targets, negatives, row_weight, boundary, tile_index, adjacency, w_proj, w_gnn):
    groups = lax.axis_size("grp")
    members = lax.axis_size("dev")
    owners = groups * members
    rows = text.shape[0]
    width = w_gnn.shape[0]
    slots = 2 * rows
    capacity = slots // owners
    place = placement_matrix(targets[:, 0], owners, capacity)
    embed = jnp.dot(text, w_proj, preferred_element_type=jnp.float32).astype(jnp.bfloat16)

    def redistribute(buffer):
        moved = lax.all_to_all(
            buffer.reshape(owners, capacity, width),
            ("grp", "dev"),
            split_axis=0,
            concat_axis=0,
            tiled=True,
        )
        return moved.reshape(slots, width)

    def take_back(buffer):
        return jnp.einsum("sr,sh->rh", place, buffer, preferred_element_type=jnp.float32)

    held = redistribute(
        jnp.dot(place, embed, preferred_element_type=jnp.float32).astype(jnp.bfloat16)
    )
    edges = held[boundary[0]]
    extra = lax.all_gather(edges, "dev", axis=0, tiled=True)
    summed, before, output_rows = layer_forward(held, extra, tile_index[0], adjacency[0], w_gnn)
    graph_rows = take_back(redistribute(output_rows))
    value, pullback = jax.vjp(
        lambda first, second: contrast(first, second, negatives, row_weight),
        graph_rows,
        embed.astype(jnp.float32),
    )
    grad_rows, grad_text = pullback(jnp.float32(1.0 / rows))
    upstream = redistribute(
        jnp.dot(place, grad_rows.astype(jnp.bfloat16), preferred_element_type=jnp.float32).astype(
            jnp.bfloat16
        )
    )
    grad_gnn, local, remote = layer_backward(
        summed, before, tile_index[0], adjacency[0], w_gnn, upstream, members
    )
    own_edges = lax.psum_scatter(
        remote.astype(jnp.bfloat16), "dev", scatter_dimension=0, tiled=True
    ).astype(jnp.float32)
    grad_held = local.at[boundary[0]].add(own_edges).astype(jnp.bfloat16)
    grad_embed = (grad_text + take_back(redistribute(grad_held))).astype(jnp.bfloat16)
    grad_proj = jnp.einsum("rd,rh->dh", text, grad_embed, preferred_element_type=jnp.float32)
    total_proj, total_gnn, total_loss = lax.psum(
        (grad_proj, grad_gnn, value / rows), ("grp", "dev")
    )
    return (total_loss / owners, total_proj, total_gnn)


def solution(mesh):
    return jax.shard_map(
        body,
        mesh=mesh,
        in_specs=(
            P(("grp", "dev"), None),
            P(("grp", "dev"), None),
            P(("grp", "dev"), None),
            P(("grp", "dev"), None),
            P(("grp", "dev"), None),
            P(("grp", "dev"), None, None),
            P(("grp", "dev"), None, None, None, None),
            P(),
            P(),
        ),
        out_specs=(P(), P(), P()),
        check_vma=False,
    )
```

profile of v0, /device:TPU:1, one launch (start us, length us, event | category | flops | bytes accessed | tf_op | source)
XLA Modules:
  0.0 600.6 jit_solution(3427456962852495199)
XLA Ops:
  7.2 0.9 copy.53
  8.1 0.2 fusion.32
  8.4 0.9 fusion.34
  9.3 0.7 multiply_add_fusion.1
  10.0 3.8 fusion.8
  13.8 0.8 copy-done.2
  14.6 0.4 convolution_convert_fusion.2
  15.1 1.2 reshape.159
  16.3 11.9 %all-to-all-start = ((bf16[128,4,1024]{2,1,0:T(4,128)(2,1)}), bf16[128,4,1024]{2,1,0:T(4,128)(2,1)}, u32[]{:S(2)}, u32[]{:S(2)}) async-start(bf16[128,4,1024]{2,1,0:T(4,128)(2,1)} %reshape.159), calls=%async_computation | async-start | bytes 2097152 | tf_op jit(solution)/shard_map/all_to_all | solution.py:87
  28.4 18.7 %all-to-all-done = bf16[128,4,1024]{2,1,0:T(4,128)(2,1)} async-done(((bf16[128,4,1024]{2,1,0:T(4,128)(2,1)}), bf16[128,4,1024]{2,1,0:T(4,128)(2,1)}, u32[]{:S(2)}, u32[]{:S(2)}) %all-to-all-start) | async-done | bytes 1048608 | tf_op jit(solution)/shard_map/all_to_all | solution.py:87
  47.1 1.3 reshape.160
  48.4 1.6 gather_fusion
  50.1 49.6 %all-gather.3.cloned.1.call-done = bf16[4096,1024]{1,0:T(8,128)(2,1)} async-done(((bf16[128,1024]{1,0:T(8,128)(2,1)}), bf16[4096,1024]{1,0:T(8,128)(2,1)}) %all-gather.3.cloned.1.call-update) | async-done | bytes 8388624 | tf_op jit(solution)/shard_map/all_gather | solution.py:103
  99.7 8.1 %pad_maximum_fusion = bf16[4608,1024]{1,0:T(8,128)(2,1)} fusion(bf16[4096,1024]{1,0:T(8,128)(2,1)} %all-gather.3.cloned.1.call-done, bf16[512,1024]{1,0:T(8,128)(2,1)S(1)} %reshape.160), kind=kLoop, calls=%fused_computation.6 | loop fusion | flops 18874368 | bytes 18874368 | tf_op jit(solution)/shard_map/concatenate | solution.py:37
  107.9 6.6 %gather_fusion.1 = bf16[16,128,1024]{2,1,0:T(8,128)(2,1)} fusion(bf16[36,128,1024]{2,1,0:T(8,128)(2,1)} %bitcast.79, s32[1024]{0:T(1024)S(1)} %pad_clamp_fusion), kind=kCustom, calls=%fused_computation.1 | custom fusion | bytes 8388672 | tf_op jit(solution)/shard_map/gather | solution.py:38
  114.4 2.9 bitcast_convert_fusion
  117.4 2.7 multiply_convert_fusion.1
  120.1 1.2 reshape.162
  121.3 7.4 %all-to-all-start.1 = ((bf16[128,4,1024]{2,1,0:T(4,128)(2,1)}), bf16[128,4,1024]{2,1,0:T(4,128)(2,1)S(1)}, u32[]{:S(2)}, u32[]{:S(2)}) async-start(bf16[128,4,1024]{2,1,0:T(4,128)(2,1)} %reshape.162), calls=%async_computation.1 | async-start | bytes 2097152 | tf_op jit(solution)/shard_map/all_to_all | solution.py:87
  128.7 0.3 reduce-scatter.2.cloned.1.call-start
  129.1 0.1 copy.55
  129.2 0.1 reshape.191
  129.4 0.1 copy.57
  129.6 0.1 reshape.205
  129.7 18.1 %all-to-all-done.1 = bf16[128,4,1024]{2,1,0:T(4,128)(2,1)S(1)} async-done(((bf16[128,4,1024]{2,1,0:T(4,128)(2,1)}), bf16[128,4,1024]{2,1,0:T(4,128)(2,1)S(1)}, u32[]{:S(2)}, u32[]{:S(2)}) %all-to-all-start.1) | async-done | bytes 1048608 | tf_op jit(solution)/shard_map/all_to_all | solution.py:87
  147.9 1.1 reshape.163
  149.0 1.8 multiply_reduce_fusion.1
  150.8 1.4 fusion.7
  152.1 2.2 fusion.2
  154.3 16.6 %gather_fusion.2 = f32[2048]{0:T(1024)S(1)} fusion(f32[256,256]{1,0:T(8,128)S(1)} %fusion.2, s32[2048]{0:T(1024)S(1)} %reshape.191), kind=kCustom, calls=%fused_computation.2 | custom fusion | bytes 32768 | tf_op jit(solution)/shard_map/jvp(jit(take_along_axis))/gather | solution.py:27
  171.2 0.1 copy.58
  171.4 0.1 reshape.207
  171.5 15.1 %scatter_custom_fusion.1 = f32[65536]{0:T(1024)} fusion(s32[2048]{0:T(1024)S(1)} %reshape.205, f32[2048]{0:T(1024)S(1)} %reshape.207, f32[]{:T(128)} %constant.24.clone.1), kind=kCustom, calls=%fused_computation.64 | custom fusion | flops 2048 | bytes 262148
  186.6 1.0 reshape.173
  187.6 0.6 negate_multiply_fusion
  188.2 2.6 multiply_reduce_fusion
  190.9 1.6 convolution_convert_fusion.1
  192.5 2.3 reshape.165
  194.7 25.4 %all_to_all.20 = bf16[128,4,1024]{2,1,0:T(4,128)(2,1)} all-to-all(bf16[128,4,1024]{2,1,0:T(4,128)(2,1)} %reshape.165), channel_id=1, replica_groups=mesh['grp'=4,'dev'=32] {'grp','dev'}, dimensions={0} | all-to-all | bytes 2097152 | tf_op jit(solution)/shard_map/all_to_all | solution.py:87
  220.2 2.4 reshape.174
  222.6 3.0 multiply_convert_fusion
  225.6 1.3 convolution_convert_fusion
  227.0 4.7 convolution_bitcast_fusion.2
  231.7 10.3 %copy.60 = f32[4,4,128,1024]{3,1,0,2:T(4,128)} copy(f32[4,4,128,1024]{2,3,1,0:T(8,128)} %convolution_bitcast_fusion.2) | data formatting | bytes 16777216 | tf_op jit(solution)/shard_map/bkij,bih->bkjh/dot_general | solution.py:60
  242.0 13.1 %convolution_bitcast_fusion = f32[36,128,1024]{2,0,1:T(8,128)S(1)} fusion(f32[4,4,128,1024]{3,1,0,2:T(4,128)} %copy.60, s32[4,4]{1,0:T(4,128)S(1)} %bitcast.92), kind=kOutput, calls=%fused_computation.7 | convolution fusion | flops 905970240 | bytes 27263040 | tf_op jit(solution)/shard_map/tbk,bkjh->tjh/dot_general | solution.py:69
  255.1 7.0 %copy-done.6 = f32[36,128,1024]{2,0,1:T(8,128)} copy-done((f32[36,128,1024]{2,0,1:T(8,128)}, f32[36,128,1024]{2,0,1:T(8,128)S(1)}, u32[]{:S(2)}) %copy-start.6) | copy-done | bytes 18874392
  262.1 5.2 slice.28
  267.3 11.4 %copy.62 = bf16[32,128,1024]{2,1,0:T(8,128)(2,1)} copy(bf16[32,128,1024]{2,0,1:T(8,128)(2,1)} %slice.28) | data formatting | bytes 16777216 | tf_op jit(solution)/shard_map/slice | solution.py:71
  278.7 2.6 slice.24
  281.3 2.5 copy.61
  283.8 82.2 %reduce-scatter.2.cloned.1.call-done = bf16[128,1024]{1,0:T(8,128)(2,1)} async-done(((bf16[4096,1024]{1,0:T(8,128)(2,1)}), bf16[128,1024]{1,0:T(8,128)(2,1)}) %reduce-scatter.2.cloned.1.call-update) | async-done | bytes 262160 | tf_op jit(solution)/shard_map/reduce_scatter | solution.py:120
  366.1 4.9 scatter_custom_fusion
  371.0 2.8 convert_element_type.78
  373.8 2.4 reshape.168
  376.1 9.7 %all-to-all-start.3 = ((bf16[128,4,1024]{2,1,0:T(4,128)(2,1)}), bf16[128,4,1024]{2,1,0:T(4,128)(2,1)}, u32[]{:S(2)}, u32[]{:S(2)}) async-start(bf16[128,4,1024]{2,1,0:T(4,128)(2,1)} %reshape.168), calls=%async_computation.4 | async-start | bytes 2097152 | tf_op jit(solution)/shard_map/all_to_all | solution.py:87
  385.9 2.3 fusion.9
  388.2 4.6 fusion.52
  392.8 11.8 %all-to-all-done.3 = bf16[128,4,1024]{2,1,0:T(4,128)(2,1)} async-done(((bf16[128,4,1024]{2,1,0:T(4,128)(2,1)}), bf16[128,4,1024]{2,1,0:T(4,128)(2,1)}, u32[]{:S(2)}, u32[]{:S(2)}) %all-to-all-start.3) | async-done | bytes 1048608 | tf_op jit(solution)/shard_map/all_to_all | solution.py:87
  404.6 1.5 reshape.169
  406.2 6.4 %convolution_bitcast_fusion.1 = f32[2048,1024]{0,1:T(8,128)} fusion(bf16[256,2048]{1,0:T(8,128)(2,1)} %param.9, bf16[512,1024]{1,0:T(8,128)(2,1)S(1)} %reshape.169, bf16[256,1024]{1,0:T(8,128)(2,1)S(1)} %copy-done.3, f32[256,1024]{1,0:T(8,128)S(1)} %copy-done.8, f32[256]{0:T(256)S(1)} %multiply_multiply_fusion.1, f32[256]{0:T(256)S(1)} %add_rsqrt_fusion, ...), kind=kOutput, calls=%fused_computation.8 | convolution fusion | flops 1344143360 | bytes 12061696 | tf_op jit(solution)/shard_map/rd,rh->dh/dot_general | solution.py:125
  413.2 63.5 %psum.21 = f32[]{:T(128)} all-reduce(f32[]{:T(128)S(6)} %div.24), channel_id=1, replica_groups=mesh['grp'=4,'dev'=32] {'grp','dev'}, use_global_device_ids=true, to_apply=%region_8.9 | all-reduce | flops 1 | bytes 8 | tf_op jit(solution)/shard_map/psum | solution.py:126
  477.4 101.1 %all-reduce.3.cloned.1.call-done = (f32[2048,1024]{0,1:T(8,128)}, f32[1024,1024]{1,0:T(8,128)}) async-done(((f32[2048,1024]{0,1:T(8,128)}, f32[1024,1024]{1,0:T(8,128)}), (f32[2048,1024]{0,1:T(8,128)}, f32[1024,1024]{1,0:T(8,128)})) %all-reduce.3.cloned.1.call-update) | async-done | bytes 12582928 | tf_op jit(solution)/shard_map/psum | solution.py:126
  578.5 9.2 %copy.63 = f32[2048,1024]{1,0:T(8,128)} copy(f32[2048,1024]{0,1:T(8,128)} %get-tuple-element.18) | data formatting | bytes 16777216
  587.8 4.9 copy.72
  (60 shorter events, 0.8 us)
Async XLA Ops:
  7.2 110.2 %copy-start = (bf16[1024,1024]{1,0:T(8,128)(2,1)S(1)}, bf16[1024,1024]{1,0:T(8,128)(2,1)}, u32[]{:S(2)}) copy-start(bf16[1024,1024]{1,0:T(8,128)(2,1)} %param.17) | copy-start | bytes 6291460
  13.8 0.8 copy-start.2
  13.8 14.5 %copy-start.15 = (s32[1,128]{1,0:T(1,128)S(1)}, s32[1,128]{1,0:T(1,128)}, u32[]{:S(2)}) copy-start(s32[1,128]{1,0:T(1,128)} %param.13) | copy-start | bytes 1540
  15.1 34.9 %copy-start.13 = (s32[1,4,4]{2,1,0:T(4,128)S(1)}, s32[1,4,4]{2,1,0:T(4,128)}, u32[]{:S(2)}) copy-start(s32[1,4,4]{2,1,0:T(4,128)} %param.14) | copy-start | bytes 196
  16.3 30.8 %all-to-all-start = ((bf16[128,4,1024]{2,1,0:T(4,128)(2,1)}), bf16[128,4,1024]{2,1,0:T(4,128)(2,1)}, u32[]{:S(2)}, u32[]{:S(2)}) async-start(bf16[128,4,1024]{2,1,0:T(4,128)(2,1)} %reshape.159), calls=%async_computation | async-start | bytes 2097152 | tf_op jit(solution)/shard_map/all_to_all | solution.py:87
  28.3 71.5 %all-gather.3.cloned.1.call-start = ((), (), s32[]{:S(2)}) async-start(), calls=%async_computation.6 | async-start | bytes 8650752 | tf_op jit(solution)/shard_map/all_gather | solution.py:103
  107.9 6.6 %copy-start.9 = (bf16[1,4,4,128,128]{4,3,2,1,0:T(8,128)(2,1)S(1)}, bf16[1,4,4,128,128]{4,3,2,1,0:T(8,128)(2,1)}, u32[]{:S(2)}) copy-start(bf16[1,4,4,128,128]{4,3,2,1,0:T(8,128)(2,1)} %param.15) | copy-start | bytes 1572868
  117.3 2.8 copy-start.4
  120.1 8.9 %copy-start.11 = (s32[256,8]{0,1:T(8,128)S(1)}, s32[256,8]{0,1:T(8,128)}, u32[]{:S(2)}) copy-start(s32[256,8]{0,1:T(8,128)} %param.11) | copy-start | bytes 24580
  120.1 9.2 %copy-start.14 = (s32[2]{0:T(128)S(1)}, s32[2]{0:T(128)}, u32[]{:S(2)}) copy-start(s32[2]{0:T(128)} %constant.66) | copy-start | bytes 28
  120.1 9.6 %copy-start.12 = (f32[256,1]{0,1:T(1,128)S(1)}, f32[256,1]{0,1:T(1,128)}, u32[]{:S(2)}) copy-start(f32[256,1]{0,1:T(1,128)} %param.12) | copy-start | bytes 3076
  121.3 26.5 %all-to-all-start.1 = ((bf16[128,4,1024]{2,1,0:T(4,128)(2,1)}), bf16[128,4,1024]{2,1,0:T(4,128)(2,1)S(1)}, u32[]{:S(2)}, u32[]{:S(2)}) async-start(bf16[128,4,1024]{2,1,0:T(4,128)(2,1)} %reshape.162), calls=%async_computation.1 | async-start | bytes 2097152 | tf_op jit(solution)/shard_map/all_to_all | solution.py:87
  128.7 237.4 %reduce-scatter.2.cloned.1.call-start = ((), (), s32[]{:S(2)}) async-start(), calls=%async_computation.5 | async-start | bytes 8650752 | tf_op jit(solution)/shard_map/reduce_scatter | solution.py:120
  225.5 1.3 copy-start.7
  225.5 1.4 copy-start.10
  255.1 7.0 %copy-start.6 = (f32[36,128,1024]{2,0,1:T(8,128)}, f32[36,128,1024]{2,0,1:T(8,128)S(1)}, u32[]{:S(2)}) copy-start(f32[36,128,1024]{2,0,1:T(8,128)S(1)} %convolution_bitcast_fusion) | copy-start | bytes 56623108
  371.0 14.9 %copy-start.3 = (bf16[256,1024]{1,0:T(8,128)(2,1)S(1)}, bf16[256,1024]{1,0:T(8,128)(2,1)}, u32[]{:S(2)}) copy-start(bf16[256,1024]{1,0:T(8,128)(2,1)} %copy-done.2) | copy-start | bytes 1572868
  373.8 14.4 %copy-start.5 = (bf16[4,1024,128]{1,2,0:T(8,128)(2,1)S(1)}, bf16[4,1024,128]{1,2,0:T(8,128)(2,1)}, u32[]{:S(2)}) copy-start(bf16[4,1024,128]{1,2,0:T(8,128)(2,1)} %copy-done.4) | copy-start | bytes 3145732
  376.1 28.5 %all-to-all-start.3 = ((bf16[128,4,1024]{2,1,0:T(4,128)(2,1)}), bf16[128,4,1024]{2,1,0:T(4,128)(2,1)}, u32[]{:S(2)}, u32[]{:S(2)}) async-start(bf16[128,4,1024]{2,1,0:T(4,128)(2,1)} %reshape.168), calls=%async_computation.4 | async-start | bytes 2097152 | tf_op jit(solution)/shard_map/all_to_all | solution.py:87
  385.8 192.7 %all-reduce.3.cloned.1.call-start = ((), (), s32[]{:S(2)}) async-start(), calls=%async_computation.7 | async-start | bytes 25165824 | tf_op jit(solution)/shard_map/psum | solution.py:126
  388.1 18.0 %copy-start.8 = (f32[256,1024]{1,0:T(8,128)S(1)}, f32[256,1024]{1,0:T(8,128)}, u32[]{:S(2)}) copy-start(f32[256,1024]{1,0:T(8,128)} %get-tuple-element.33) | copy-start | bytes 3145732
  587.8 4.9 copy-start.1
Sparse Core Ops, SparseCore 0:
  50.1 49.5 all-gather.2
  278.8 87.1 reduce-scatter.1
  412.7 165.8 all-reduce.2
where the time goes:
time: 608 us; the launch traced here: 601 us
  waiting for transfers between devices  282 us (46%)
  local copies, waits for them, and re-layouts  95.3 us (16%)
  blocking collectives  88.9 us (15%)
  matrix products  50.5 us (8%)
  other arithmetic  37.9 us (6%)
  starting transfers between devices  29.4 us (5%)
  between operations  16.8 us (3%)
    psum x1, waiting for transfers between devices, body(): lax.psum((grad_proj, grad_gnn, value / rows), ('grp', 'dev'))  101 us
    reduce_scatter x1, waiting for transfers between devices, body(): lax.psum_scatter(remote.astype(jnp.bfloat16), 'dev', scatter_dimension=0,...  82.2 us
    psum x1, blocking collectives, body(): lax.psum((grad_proj, grad_gnn, value / rows), ('grp', 'dev'))  63.5 us
    all_gather x1, waiting for transfers between devices, body(): extra = lax.all_gather(edges, 'dev', axis=0, tiled=True)  49.6 us
    all_to_all x3, waiting for transfers between devices, redistribute(): lax.all_to_all(buffer.reshape(owners, capacity, width), ('grp', 'dev'), s...  48.7 us
    all_to_all x3, starting transfers between devices, redistribute(): lax.all_to_all(buffer.reshape(owners, capacity, width), ('grp', 'dev'), s...  29 us
    all_to_all x1, blocking collectives, redistribute(): lax.all_to_all(buffer.reshape(owners, capacity, width), ('grp', 'dev'), s...  25.4 us
    unnamed x37, local copies, waits for them, and re-layouts  22.4 us
  transfers between devices with their start and end apart: 6, of which 6 were waited for; matrix products, arithmetic and copies ran while one was open for 2% of the time, Pallas kernels for 0%

commit v1 on v0

v1 whole, which is shorter than its diff:
```python
import functools

import jax
import jax.numpy as jnp
from jax import lax
from jax.experimental import pallas as pl
from jax.experimental.pallas import tpu as pltpu
from jax.sharding import Mesh, PartitionSpec as P

logit_scale = 8.0
logit_bias = -4.0
norm_floor = 1e-06
CAP = 4
BLOCKS = 4
PICKS = 4
CHIP = 2
RING = 4
ALL = ("y", "x", "z", "core")
CHIPS = ("y", "x", "z")
MEMBERS = ("x", "z", "core")

f32 = jnp.float32
bf16 = jnp.bfloat16
VMEM = pl.BlockSpec(memory_space=pltpu.VMEM)
SMEM = pl.BlockSpec(memory_space=pltpu.SMEM)
ANYWHERE = pl.BlockSpec(memory_space=pl.ANY)


def params(mib=36):
    return pltpu.CompilerParams(vmem_limit_bytes=mib * 2**20)


def cost(flops, nbytes):
    return pl.CostEstimate(flops=int(flops), bytes_accessed=int(nbytes), transcendentals=0)


def dot(a, b):
    return jnp.dot(a, b, preferred_element_type=f32)


def dot_ta(a, b):
    return lax.dot_general(a, b, (((0,), (0,)), ((), ())), preferred_element_type=f32)


def dot_tb(a, b):
    return lax.dot_general(a, b, (((1,), (1,)), ((), ())), preferred_element_type=f32)


def iota(shape, axis):
    return lax.broadcasted_iota(jnp.int32, shape, axis)


def ones_where(mask):
    return jnp.where(mask, 1.0, 0.0).astype(bf16)


def halves(x):
    high = x.astype(bf16)
    return high, (x - high.astype(f32)).astype(bf16)


def row_to_matrix(row):
    n = row.shape[1]
    return jnp.broadcast_to(row, (n, n)).T


def ranks(t_row):
    n = t_row.shape[1]
    across = jnp.broadcast_to(t_row.astype(f32), (n, n))
    down = across.T
    same = across == down
    i0, i1 = iota((n, n), 0), iota((n, n), 1)
    rank_row = jnp.sum(jnp.where(same & (i0 < i1), 1.0, 0.0), axis=0, keepdims=True)
    rank_col = jnp.sum(jnp.where(same & (i1 < i0), 1.0, 0.0), axis=1, keepdims=True)
    return (
        rank_row.astype(jnp.int32),
        rank_col.astype(jnp.int32),
        down[:, :1].astype(jnp.int32),
    )


def wide_slot(t, rank, half):
    return t * (2 * CAP) + half * CAP + rank


def spread(t_row, rank_row, first, second, rows):
    n = t_row.shape[1]
    at = iota((rows, n), 0)
    place = jnp.concatenate(
        [ones_where(at == wide_slot(t_row, rank_row, h)) for h in range(2)], axis=1
    )
    return dot(place, jnp.concatenate([first, second], axis=0))


def collect(t_col, rank_col, buffer, half):
    n, rows = t_col.shape[0], buffer.shape[0]
    return dot(ones_where(iota((n, rows), 1) == wide_slot(t_col, rank_col, half)), buffer)


def weave(tile):
    i, j = iota((2 * tile, 2 * tile), 0), iota((2 * tile, 2 * tile), 1)
    source = ((i // CAP) % 2) * tile + (i // (2 * CAP)) * CAP + i % CAP
    return ones_where(j == source)


def unweave(tile):
    i, j = iota((2 * tile, 2 * tile), 0), iota((2 * tile, 2 * tile), 1)
    source = ((j // CAP) % 2) * tile + (j // (2 * CAP)) * CAP + j % CAP
    return ones_where(i == source)


def place_kernel(first, second, t_row, sent):
    rank_row, _, _ = ranks(t_row[...])
    sent[...] = spread(t_row[...], rank_row, first[...], second[...], sent.shape[0]).astype(bf16)


def place_rows(text, t_row):
    rows, depth = text.shape
    steps = 4
    piece = depth // 2 // steps
    return pl.pallas_call(
        place_kernel,
        grid=(steps,),
        in_specs=[
            pl.BlockSpec((rows, piece), lambda i: (0, i)),
            pl.BlockSpec((rows, piece), lambda i: (0, i + steps)),
            pl.BlockSpec((1, rows), lambda i: (0, 0)),
        ],
        out_specs=pl.BlockSpec((4 * rows, piece), lambda i: (0, i)),
        out_shape=jax.ShapeDtypeStruct((4 * rows, depth // 2), bf16),
        compiler_params=params(),
        cost_estimate=cost(8 * rows * rows * depth, 3 * 2**20),
    )(text, text, t_row)


def embed_kernel(text, w, embed, total):
    step = pl.program_id(0)

    @pl.when(step == 0)
    def _():
        total[...] = jnp.zeros_like(total)

    total[...] += dot(text[...], w[...])

    @pl.when(step == pl.num_programs(0) - 1)
    def _():
        embed[...] = total[...].astype(bf16)


def embed_rows(text, w_proj):
    rows, depth = text.shape
    width = w_proj.shape[1]
    steps = 4
    piece = depth // steps
    return pl.pallas_call(
        embed_kernel,
        grid=(steps,),
        in_specs=[
            pl.BlockSpec((rows, piece), lambda i: (0, i)),
            pl.BlockSpec((piece, width), lambda i: (i, 0)),
        ],
        out_specs=pl.BlockSpec((rows, width), lambda i: (0, 0)),
        out_shape=jax.ShapeDtypeStruct((rows, width), bf16),
        scratch_shapes=[pltpu.VMEM((rows, width), f32)],
        compiler_params=params(),
        cost_estimate=cost(2 * rows * depth * width, 6 * 2**20),
    )(text, w_proj)


def edges_kernel(got, boundary, edges, held, sem):
    slot = row_to_matrix(boundary[...].astype(f32))[:, :1].astype(jnp.int32)
    at = iota((slot.shape[0], got.shape[0]), 1)
    half = got.shape[1]
    for h in range(2):
        pick = ones_where(at == wide_slot(slot // CAP, slot % CAP, h))
        held[:, h * half:(h + 1) * half] = dot(pick, got[...]).astype(bf16)
    copy = pltpu.make_async_copy(held, edges, sem)
    copy.start()
    copy.wait()


def edge_rows(got, boundary):
    shape = (boundary.shape[1], 2 * got.shape[1])
    return pl.pallas_call(
        edges_kernel,
        in_specs=[VMEM, VMEM],
        out_specs=ANYWHERE,
        out_shape=jax.ShapeDtypeStruct(shape, bf16),
        scratch_shapes=[pltpu.VMEM(shape, bf16), pltpu.SemaphoreType.DMA],
        compiler_params=params(),
        cost_estimate=cost(2 * shape[0] * shape[1] * got.shape[0], 3 * 2**20),
    )(got, boundary)


def hold_kernel(got, out):
    tile, half = out.shape[1], got.shape[1]
    both = dot(unweave(tile), got[...]).astype(bf16)
    out[0, :, :half] = both[:tile]
    out[0, :, half:] = both[tile:]


def hold_rows(got):
    rows, half = got.shape
    tile = rows // (2 * BLOCKS)
    return pl.pallas_call(
        hold_kernel,
        grid=(BLOCKS,),
        in_specs=[pl.BlockSpec((2 * tile, half), lambda i: (i, 0))],
        out_specs=pl.BlockSpec((1, tile, 2 * half), lambda i: (i, 0, 0)),
        out_shape=jax.ShapeDtypeStruct((BLOCKS, tile, 2 * half), bf16),
        compiler_params=params(),
        cost_estimate=cost(4 * tile * rows * half, 4 * 2**20),
    )(got)


def forward_kernel(
    index, extra, local, adj, w_proj, w_gnn, texts, summed, slope_factor, sent,
    src, proj, gnn, texts_v, summed_v, slope_v, sent_v, sems, more,
):
    tile = extra.shape[1]
    half = sent.shape[1]

    def place(n):
        return src.at[n // PICKS, pl.ds(n % PICKS * tile, tile), :]

    def start(n):
        t = index[0, n]

        @pl.when(t < BLOCKS)
        def _():
            pltpu.make_async_copy(local.at[t], place(n), sems.at[n]).start()

        @pl.when(t >= BLOCKS)
        def _():
            pltpu.make_async_copy(extra.at[t - BLOCKS], place(n), sems.at[n]).start()

    load_proj = pltpu.make_async_copy(w_proj, proj, more.at[0])
    load_gnn = pltpu.make_async_copy(w_gnn, gnn, more.at[1])
    stores = []

    def store(held, out, rows):
        copy = pltpu.make_async_copy(
            held.at[rows, :], out.at[rows, :], more.at[2 + len(stores)]
        )
        copy.start()
        stores.append(copy)

    count = BLOCKS * PICKS
    for n in range(count // 2):
        start(n)
    load_proj.start()
    load_gnn.start()
    for n in range(count // 2, count):
        start(n)
    order = weave(tile)
    for pair in range(BLOCKS // 2):
        rows = pl.ds(2 * pair * tile, 2 * tile)
        for b in (2 * pair, 2 * pair + 1):
            for p in range(PICKS):
                n = b * PICKS + p
                pltpu.make_async_copy(extra.at[0], place(n), sems.at[n]).wait()
            weights = jnp.concatenate([adj[b, p] for p in range(PICKS)], axis=1)
            texts_v[pl.ds(b * tile, tile), :] = dot(weights, src[b]).astype(bf16)
        store(texts_v, texts, rows)
        if pair == 0:
            load_proj.wait()
        summed_v[rows, :] = dot(texts_v[rows, :], proj[...]).astype(bf16)
        store(summed_v, summed, rows)
        if pair == 0:
            load_gnn.wait()
        before = dot(summed_v[rows, :], gnn[...])
        sigma = jax.nn.sigmoid(before)
        out = (before * sigma).astype(bf16)
        slope_v[rows, :] = (sigma * (1.0 + before * (1.0 - sigma))).astype(bf16)
        store(slope_v, slope_factor, rows)
        for i in range(2):
            block = out[i * tile:(i + 1) * tile]
            stacked = jnp.concatenate([block[:, :half], block[:, half:]], axis=0)
            at = pl.ds(2 * tile * (2 * pair + i), 2 * tile)
            sent_v[at, :] = dot(order, stacked).astype(bf16)
            store(sent_v, sent, at)
    for copy in stores:
        copy.wait()


def forward(index, extra, local, adj, w_proj, w_gnn):
    _, tile, depth = extra.shape
    slots, width = BLOCKS * tile, w_gnn.shape[0]
    shapes = [(slots, depth), (slots, width), (slots, width), (2 * slots, width // 2)]
    return pl.pallas_call(
        forward_kernel,
        in_specs=[SMEM, ANYWHERE, ANYWHERE, VMEM, ANYWHERE, ANYWHERE],
        out_specs=[ANYWHERE] * 4,
        out_shape=[jax.ShapeDtypeStruct(shape, bf16) for shape in shapes],
        scratch_shapes=[
            pltpu.VMEM((BLOCKS, PICKS * tile, depth), bf16),
            pltpu.VMEM(w_proj.shape, bf16),
            pltpu.VMEM(w_gnn.shape, bf16),
            *[pltpu.VMEM(shape, bf16) for shape in shapes],
            pltpu.SemaphoreType.DMA((BLOCKS * PICKS,)),
            pltpu.SemaphoreType.DMA((12,)),
        ],
        compiler_params=params(56),
        cost_estimate=cost(2 * slots * depth * width + 2 * adj.size * depth, 22 * 2**20),
    )(index, extra, local, adj, w_proj, w_gnn)


def loss_kernel(
    core, back, embed, t_row, negatives, weights, sent_out, text_keep, text_send, sent, both, sems
):
    rank_row, rank_col, t_col = ranks(t_row[...])
    buffer = back[...]
    first = collect(t_col, rank_col, buffer, 0)
    second = collect(t_col, rank_col, buffer, 1)
    graph = jnp.concatenate([first, second], axis=1)
    graph_b = graph.astype(bf16)
    text_b = embed[...]
    text = text_b.astype(f32)
    n = graph.shape[0]
    scale_g = lax.rsqrt(jnp.sum(graph * graph, axis=1, keepdims=True) + norm_floor)
    scale_t = lax.rsqrt(jnp.sum(text * text, axis=1, keepdims=True) + norm_floor)
    across_g = jnp.broadcast_to(scale_g, (n, n)).T
    similar = dot_tb(text_b, graph_b) * scale_t * across_g
    i0, i1 = iota((n, n), 0), iota((n, n), 1)
    count = jnp.zeros((n, n), f32)
    for m in range(negatives.shape[0]):
        count = count + jnp.where(i0 == negatives[m:m + 1, :], 1.0, 0.0)
    same = i0 == i1
    logit = logit_scale * similar + logit_bias
    tail = jnp.log1p(jnp.exp(-jnp.abs(logit)))
    plus = jnp.maximum(logit, 0.0) + tail
    minus = jnp.maximum(-logit, 0.0) + tail
    weight = weights[...]
    per_pair = weight * (count * plus + jnp.where(same, minus, 0.0))
    total = jnp.sum(per_pair, keepdims=True)
    sigma = jax.nn.sigmoid(logit)
    slope = (weight * (logit_scale / n)) * (count * sigma - jnp.where(same, 1.0 - sigma, 0.0))
    to_graph_hi, to_graph_lo = halves(slope * scale_t)
    unit_grad = dot_ta(to_graph_hi, text_b) + dot_ta(to_graph_lo, text_b)
    unit = graph * scale_g
    grad = scale_g * (unit_grad - unit * jnp.sum(unit * unit_grad, axis=1, keepdims=True))
    to_text_hi, to_text_lo = halves(slope * across_g)
    unit_grad = dot(to_text_hi, graph_b) + dot(to_text_lo, graph_b)
    unit = text * scale_t
    grad_text = (
        scale_t * (unit_grad - unit * jnp.sum(unit * unit_grad, axis=1, keepdims=True))
    ).astype(bf16)
    grad_b = grad.astype(bf16)
    half = grad.shape[1] // 2
    both[0] = grad_text[:, :half]
    both[1] = grad_text[:, half:]
    copies = [
        pltpu.make_async_copy(both.at[core[0]], text_keep, sems.at[0]),
        pltpu.make_async_copy(both.at[1 - core[0]], text_send, sems.at[1]),
        pltpu.make_async_copy(sent, sent_out, sems.at[2]),
    ]
    copies[0].start()
    copies[1].start()
    sent[:, :half] = spread(
        t_row[...], rank_row, grad_b[:, :half], grad_b[:, half:], sent.shape[0]
    ).astype(bf16)
    shape = (sent.shape[0], sent.shape[1] - half)
    whole = jnp.broadcast_to(total, shape)
    high = whole.astype(bf16).astype(f32)
    mid = (whole - high).astype(bf16).astype(f32)
    lane = jnp.where(iota(shape, 0) % (2 * CAP) == 0, iota(shape, 1), 3)
    parts = jnp.where(lane == 0, high, jnp.where(lane == 1, mid, whole - high - mid))
    sent[:, half:] = jnp.where(lane < 3, parts, 0.0).astype(bf16)
    copies[2].start()
    for copy in copies:
        copy.wait()


def loss_side(core, back, embed, t_row, negatives, weights):
    part = jax.ShapeDtypeStruct((embed.shape[0], embed.shape[1] // 2), bf16)
    shape = (back.shape[0], back.shape[1] + 128)
    return pl.pallas_call(
        loss_kernel,
        in_specs=[SMEM] + [VMEM] * 5,
        out_specs=[ANYWHERE] * 3,
        out_shape=[jax.ShapeDtypeStruct(shape, bf16), part, part],
        scratch_shapes=[
            pltpu.VMEM(shape, bf16),
            pltpu.VMEM((2, *part.shape), bf16),
            pltpu.SemaphoreType.DMA((3,)),
        ],
        compiler_params=params(),
        cost_estimate=cost(8 * 2**30, 4 * 2**20),
    )(core, back, embed, t_row, negatives, weights)


def slope_kernel(loss_scale, core, back, slope_factor, slope, keep, send, loss):
    k = core[0]
    half = keep.shape[1]
    tile = slope.shape[0] // BLOCKS
    order = unweave(tile)
    for b in range(BLOCKS):
        rows = pl.ds(b * tile, tile)
        stacked = dot(order, back[pl.ds(2 * tile * b, 2 * tile), :half])
        upstream = jnp.concatenate([stacked[:tile], stacked[tile:]], axis=1)
        slope[rows, :] = (upstream * slope_factor[rows, :].astype(f32)).astype(bf16)
    for member, out in ((k, keep), (1 - k, send)):
        out[...] = slope[:, pl.ds(pl.multiple_of(member * half, half), half)]
    loss[...] = jnp.broadcast_to(
        jnp.sum(back[:, half:].astype(f32), keepdims=True) * loss_scale, loss.shape
    )


def slopes(core, back, slope_factor, loss_scale):
    slots, width = slope_factor.shape
    part = jax.ShapeDtypeStruct((slots, width // 2), bf16)
    return pl.pallas_call(
        functools.partial(slope_kernel, loss_scale),
        in_specs=[SMEM] + [VMEM] * 2,
        out_specs=[VMEM] * 4,
        out_shape=[
            jax.ShapeDtypeStruct((slots, width), bf16),
            part,
            part,
            jax.ShapeDtypeStruct((1, 128), f32),
        ],
        compiler_params=params(),
        cost_estimate=cost(2 * slots * slots * width, 4 * 2**20),
    )(core, back, slope_factor)


def grad_sum_kernel(core, slope, w, keep, send):
    half = keep.shape[1]
    for member, out in ((core[0], keep), (1 - core[0], send)):
        rows = pl.ds(pl.multiple_of(member * half, half), half)
        out[...] = dot_tb(slope[...], w[rows, :]).astype(bf16)


def grad_sums(core, slope, w):
    slots, width = slope.shape
    part = jax.ShapeDtypeStruct((slots, width // 2), bf16)
    return pl.pallas_call(
        grad_sum_kernel,
        in_specs=[SMEM] + [VMEM] * 2,
        out_specs=[VMEM] * 2,
        out_shape=[part, part],
        compiler_params=params(),
        cost_estimate=cost(2 * slots * w.size, 4 * 2**20),
    )(core, slope, w)


def layer_weights_kernel(s0, s1, y0, y1, out):
    out[...] = (dot_ta(s0[...], y0[...]) + dot_ta(s1[...], y1[...])).astype(bf16)


def proj_weights_kernel(x0, x1, t0, t1, y0, y1, g0, g1, before, out):
    out[...] = (
        dot_ta(x0[...], y0[...])
        + dot_ta(x1[...], y1[...])
        + dot_ta(t0[...], g0[...])
        + dot_ta(t1[...], g1[...])
    ).astype(bf16)


def columns_of(array, piece):
    return pl.BlockSpec((array.shape[0], piece), lambda i: (0, i))


def all_of(array):
    return pl.BlockSpec(array.shape, lambda i: (0, 0))


def layer_weights(summed, y, depth):
    width, half = summed[0].shape[1], y[0].shape[1]
    piece = width // 2
    return pl.pallas_call(
        layer_weights_kernel,
        grid=(width // piece,),
        in_specs=[columns_of(array, piece) for array in summed]
        + [all_of(array) for array in y],
        out_specs=pl.BlockSpec((piece, half), lambda i: (i, 0)),
        out_shape=jax.ShapeDtypeStruct((width + depth, half), bf16),
        compiler_params=params(),
        cost_estimate=cost(4 * width * y[0].size, 5 * 2**20),
    )(*summed, *y)


def proj_weights(texts, text, y, g, before):
    depth, half = texts[0].shape[1], y[0].shape[1]
    width = before.shape[0] - depth
    piece = width // 2
    return pl.pallas_call(
        proj_weights_kernel,
        grid=(depth // piece,),
        in_specs=[columns_of(array, piece) for array in (*texts, *text)]
        + [all_of(array) for array in (*y, *g)]
        + [ANYWHERE],
        out_specs=pl.BlockSpec((piece, half), lambda i: (i + width // piece, 0)),
        out_shape=jax.ShapeDtypeStruct(before.shape, bf16),
        input_output_aliases={8: 0},
        compiler_params=params(),
        cost_estimate=cost(4 * depth * y[0].size, 10 * 2**20),
    )(*texts, *text, *y, *g, before)


def pieces_kernel(pieces, out):
    total = jnp.sum(pieces[...].astype(f32), axis=0).astype(bf16)
    out[...] = jnp.broadcast_to(total[None], out.shape)


def sum_repeated(pieces):
    chips, rows, width = pieces.shape
    steps = 3
    block = pl.BlockSpec((chips, rows // steps, width), lambda i: (0, i, 0))
    return pl.pallas_call(
        pieces_kernel,
        grid=(steps,),
        in_specs=[block],
        out_specs=block,
        out_shape=jax.ShapeDtypeStruct(pieces.shape, bf16),
        compiler_params=params(),
        cost_estimate=cost(pieces.size, 4 * pieces.size),
    )(pieces)


def out_kernel(member, part, *refs):
    gnn, proj, wide, sems = refs[-4:]
    rows, half = part.shape
    count = sems.shape[0]
    piece = rows // count
    columns = pl.ds(pl.multiple_of(member[0] * half, half), half)
    copies = []
    for i in range(count):
        at = pl.ds(i * piece, piece)
        wide[at, :] = part[at, :].astype(f32)
        first = i * piece < gnn.shape[0]
        out, start = (gnn, i * piece) if first else (proj, i * piece - gnn.shape[0])
        copy = pltpu.make_async_copy(
            wide.at[at, :], out.at[pl.ds(start, piece), columns], sems.at[i]
        )
        copy.start()
        copies.append(copy)
    for copy in copies:
        copy.wait()


def write_half(member, part, width, before=()):
    rows, half = part.shape
    return pl.pallas_call(
        out_kernel,
        in_specs=[SMEM, VMEM] + [ANYWHERE] * len(before),
        out_specs=[ANYWHERE] * 2,
        out_shape=[
            jax.ShapeDtypeStruct((width, 2 * half), f32),
            jax.ShapeDtypeStruct((rows - width, 2 * half), f32),
        ],
        scratch_shapes=[pltpu.VMEM((rows, half), f32), pltpu.SemaphoreType.DMA((12,))],
        input_output_aliases={2: 0, 3: 1} if before else {},
        compiler_params=params(),
        cost_estimate=cost(0, 6 * part.size),
    )(member, part, *before)


def body(text, targets, negatives, row_weight, boundary, tile_index, adjacency, w_proj, w_gnn):
    chips = lax.axis_size("y") * lax.axis_size("x") * lax.axis_size("z")
    owners = chips * lax.axis_size("core")
    rows = text.shape[0]
    t_row = targets.reshape(1, rows)
    negative_rows = negatives.T
    weights = row_weight.reshape(1, rows)
    adjacency = adjacency[0]
    index = tile_index.reshape(1, BLOCKS * PICKS)
    core = lax.axis_index("core").reshape(1)
    together = lax.optimization_barrier

    def swap(array):
        return lax.ppermute(array, "core", [(0, 1), (1, 0)])

    def redistribute(buffer):
        return lax.all_to_all(buffer, ALL, split_axis=0, concat_axis=0, tiled=True)

    def between_chips(array):
        return lax.all_to_all(array, CHIPS, split_axis=0, concat_axis=0, tiled=True)

    got = redistribute(place_rows(text, t_row))
    edges = edge_rows(got, boundary)
    extra = lax.all_gather(edges[None], MEMBERS, axis=0, tiled=True)
    local = hold_rows(got)
    embed = embed_rows(text, w_proj)
    other_text = swap(text)
    extra, local, embed, other_text = together((extra, local, embed, other_text))
    texts, summed, slope_factor, sent = forward(index, extra, local, adjacency, w_proj, w_gnn)
    other_texts, other_summed = swap(texts), swap(summed)
    sent, text_keep, text_send = loss_side(
        core, redistribute(sent), embed, t_row, negative_rows, weights
    )
    text_got = swap(text_send)
    back, text_got = together((redistribute(sent), text_got))
    slope, slope_keep, slope_send, loss = slopes(
        core, back, slope_factor, 1.0 / (owners * rows)
    )
    slope_got = swap(slope_send)
    keep, send = grad_sums(core, slope, w_gnn)
    total = layer_weights((summed, other_summed), (slope_keep, slope_got), text.shape[1])
    total = proj_weights(
        (texts, other_texts), (text, other_text), (keep, swap(send)), (text_keep, text_got), total
    )
    pieces = between_chips(total).reshape(chips, -1, total.shape[1])
    mine = between_chips(sum_repeated(pieces).reshape(total.shape))
    theirs = swap(mine)
    width = w_gnn.shape[0]
    total_gnn, total_proj = write_half(1 - core, theirs, width, write_half(core, mine, width))
    return loss[0, 0], total_proj, total_gnn


def solution(mesh):
    groups, members = mesh.devices.shape
    fine = Mesh(mesh.devices.reshape(groups, RING, RING, members // RING**2), ALL)
    rows = P(ALL, None)
    return jax.shard_map(
        body,
        mesh=fine,
        in_specs=(
            rows,
            rows,
            rows,
            rows,
            rows,
            P(ALL, None, None),
            P(ALL, None, None, None, None),
            P(),
            P(),
        ),
        out_specs=(P(), P(), P()),
        check_vma=False,
    )
```

time: 608 us -> 318 us (0.52); the launches traced: 601 us -> 317 us
  waiting for transfers between devices: 282 us -> 101 us
  local copies, waits for them, and re-layouts: 95.3 us -> 12.6 us
  matrix products: 50.5 us -> 0 us
  blocking collectives: 88.9 us -> 129 us
  Pallas kernels: 0 us -> 40 us
  other arithmetic: 37.9 us -> 0 us
  starting transfers between devices: 29.4 us -> 20.7 us
    all_to_all x1 -> x3, blocking collectives: 25.4 us -> 129 us  [the longest x2 87.5 us: between_chips(): return lax.all_to_all(array, CHIPS, split_axis=0, concat_axis=0, tiled=True)]
    psum x1 -> x0, waiting for transfers between devices: 101 us -> none  [body(): lax.psum((grad_proj, grad_gnn, value / rows), ('grp', 'dev'))]
    reduce_scatter x1 -> x0, waiting for transfers between devices: 82.2 us -> none  [body(): lax.psum_scatter(remote.astype(jnp.bfloat16), 'dev', scatter_dimension=0,...]
    psum x1 -> x0, blocking collectives: 63.5 us -> none  [body(): lax.psum((grad_proj, grad_gnn, value / rows), ('grp', 'dev'))]
    dot_general x14 -> x0, matrix products: 50.5 us -> none  [the longest x1 13.1 us: layer_backward(): jnp.einsum('tbk,bkjh->tjh', selector, term, precision=lax.Precision.HIGHEST)]
    pallas_call x0 -> x13, Pallas kernels: none -> 40 us  [the longest x1 12.3 us: forward(): pl.pallas_call(forward_kernel, in_specs=[SMEM, ANYWHERE, ANYWHERE, VMEM,...]
    gather x8 -> x0, local copies, waits for them, and re-layouts: 25.2 us -> none  [the longest x6 17 us: contrast(): negative = jnp.take_along_axis(similar, partners, axis=1)]
    slice x4 -> x0, local copies, waits for them, and re-layouts: 21.7 us -> none  [the longest x2 16.6 us: layer_backward(): remote = grad_tiles[blocks:].reshape(members * tile_rows, width)]
  transfers between devices with their start and end apart: 6 -> 10, of which waited for: 6 -> 5; matrix products, arithmetic and copies ran while one was open for 2% -> 0% of each run, Pallas kernels for 0% -> 5%
where the time goes in v1:
time: 318 us; the launch traced here: 317 us
  blocking collectives  129 us (41%)
  waiting for transfers between devices  101 us (32%)
  Pallas kernels  40 us (13%)
  starting transfers between devices  20.7 us (7%)
  between operations  14.4 us (5%)
  local copies, waits for them, and re-layouts  12.6 us (4%)
    all_to_all x2, blocking collectives, between_chips(): return lax.all_to_all(array, CHIPS, split_axis=0, concat_axis=0, tiled=True)  87.5 us
    all_gather x1, waiting for transfers between devices, body(): extra = lax.all_gather(edges[None], MEMBERS, axis=0, tiled=True)  60.3 us
    all_to_all x1, blocking collectives, redistribute(): return lax.all_to_all(buffer, ALL, split_axis=0, concat_axis=0, tiled=True)  41.5 us
    all_to_all x2, waiting for transfers between devices, redistribute(): return lax.all_to_all(buffer, ALL, split_axis=0, concat_axis=0, tiled=True)  35.2 us
    pallas_call x1, Pallas kernels, forward(): pl.pallas_call(forward_kernel, in_specs=[SMEM, ANYWHERE, ANYWHERE, VMEM,...  12.3 us
    unnamed x46, local copies, waits for them, and re-layouts  12 us
    all_to_all x2, starting transfers between devices, redistribute(): return lax.all_to_all(buffer, ALL, split_axis=0, concat_axis=0, tiled=True)  11.9 us
    ppermute x7, starting transfers between devices, swap(): return lax.ppermute(array, 'core', [(0, 1), (1, 0)])  8.81 us
  transfers between devices with their start and end apart: 10, of which 5 were waited for; matrix products, arithmetic and copies ran while one was open for 0% of the time, Pallas kernels for 5%

profile of v1, /device:TPU:1, one launch (start us, length us, event | category | flops | bytes accessed | tf_op | source)
XLA Modules:
  0.0 317.4 jit_solution(3899888291087905527)
XLA Ops:
  7.2 0.0 all-gather.3.cloned.1.call-start
  7.2 0.0 copy-start
  7.2 1.2 copy-done
  8.4 0.7 copy-done.16
  9.1 2.6 shard_map.112
  11.7 0.0 copy-start.18
  11.7 0.0 copy-start.1
  11.7 0.0 copy-start.22
  11.7 41.5 %all_to_all.51 = bf16[128,8,1024]{2,1,0:T(8,128)(2,1)S(1)} all-to-all(bf16[128,8,1024]{2,1,0:T(8,128)(2,1)S(1)} %bitcast.21), channel_id=1, replica_groups=mesh['y'=4,'x'=4,'z'=4,'core'=2] {'y','x','z','core'}, dimensions={0} | all-to-all | bytes 4194304 | tf_op jit(solution)/shard_map/all_to_all | solution.py:575
  53.3 0.0 copy-done.18
  53.3 0.9 shard_map.113
  54.2 0.0 copy-start.5
  54.2 0.8 copy-done.5
  55.0 0.0 all-gather.3.cloned.1.call-update
  55.0 0.0 copy-done.1
  55.0 1.3 collective-permute-start
  56.4 0.0 copy-done.22
  56.4 0.6 reshape.33.index
  57.0 2.2 copy-done.2
  59.2 2.0 shard_map.115.embed
  61.2 0.0 copy-start.10
  61.2 1.3 shard_map.114.local
  62.5 0.0 copy-start.3
  62.5 1.3 copy-done.3
  63.8 0.0 collective-permute-done.t1
  63.8 60.3 %all-gather.3.cloned.1.call-done = bf16[4096,2048]{1,0:T(8,128)(2,1)} async-done(((bf16[128,2048]{1,0:T(8,128)(2,1)}), bf16[4096,2048]{1,0:T(8,128)(2,1)}) %all-gather.3.cloned.1.call-update) | async-done | bytes 16777232 | tf_op jit(solution)/shard_map/all_gather | solution.py:582
  124.1 12.3 %shard_map.116 = (bf16[512,2048]{1,0:T(8,128)(2,1)}, bf16[512,1024]{1,0:T(8,128)(2,1)}, bf16[512,1024]{1,0:T(8,128)(2,1)}, bf16[1024,512]{1,0:T(8,128)(2,1)}) custom-call(s32[1,16]{1,0:T(1,128)} %reshape.33.index, bf16[32,128,2048]{2,1,0:T(8,128)(2,1)} %bitcast.29, bf16[4,128,2048]{2,1,0:T(8,128)(2,1)} %copy-done.3, bf16[4,4,128,128]{3,2,1,0:T(8,128)(2,1)} %bitcast.31, ...), custom_call_target="tpu_custom_call" | custom-call | flops 3221225472 | bytes 23068672 | tf_op jit(solution)/shard_map/pallas_call | solution.py:290
  136.4 7.3 %all-to-all-start.1 = ((bf16[128,8,512]{2,1,0:T(8,128)(2,1)}), bf16[128,8,512]{2,1,0:T(8,128)(2,1)S(1)}, u32[]{:S(2)}, u32[]{:S(2)}) async-start(bf16[128,8,512]{2,1,0:T(8,128)(2,1)} %bitcast.30), calls=%async_computation.1 | async-start | bytes 2097152 | tf_op jit(solution)/shard_map/all_to_all | solution.py:575
  143.7 1.3 collective-permute-start.2
  145.0 17.8 %all-to-all-done.1 = bf16[128,8,512]{2,1,0:T(8,128)(2,1)S(1)} async-done(((bf16[128,8,512]{2,1,0:T(8,128)(2,1)}), bf16[128,8,512]{2,1,0:T(8,128)(2,1)S(1)}, u32[]{:S(2)}, u32[]{:S(2)}) %all-to-all-start.1) | async-done | bytes 1048608 | tf_op jit(solution)/shard_map/all_to_all | solution.py:575
  162.9 0.0 copy-start.11
  162.9 1.0 copy-done.11
  163.9 3.8 %shard_map.117 = (bf16[1024,640]{1,0:T(8,128)(2,1)S(1)}, bf16[256,512]{1,0:T(8,128)(2,1)S(1)}, bf16[256,512]{1,0:T(8,128)(2,1)S(1)}) custom-call(s32[1]{0:T(128)} %bitcast.core.member, bf16[1024,512]{1,0:T(8,128)(2,1)S(1)} %bitcast.24, bf16[256,1024]{1,0:T(8,128)(2,1)S(1)} %copy-done.11, s32[1,256]{1,0:T(1,128)S(1)} %bitcast.26, s32[8,256]{1,0:T(8,128)S(1)} %bitcast.27, ...), custom_call_target="tpu_custom_call" | custom-call | flops 8589934592 | bytes 4194304 | tf_op jit(solution)/shard_map/pallas_call | solution.py:377
  167.7 0.0 copy-start.7
  167.7 1.0 copy-done.7
  168.8 0.7 copy-done.12
  169.5 0.7 copy-done.19
  170.2 4.6 %all-to-all-start.2 = ((bf16[128,8,640]{2,1,0:T(8,128)(2,1)}), bf16[128,8,640]{2,1,0:T(8,128)(2,1)S(1)}, u32[]{:S(2)}, u32[]{:S(2)}) async-start(bf16[128,8,640]{2,1,0:T(8,128)(2,1)} %bitcast.23), calls=%async_computation.2 | async-start | bytes 2621440 | tf_op jit(solution)/shard_map/all_to_all | solution.py:575
  174.8 1.3 collective-permute-start.4
  176.1 0.1 collective-permute-start.1
  176.2 2.6 collective-permute-done.1.g1
  178.9 0.7 copy-done.14
  179.5 17.3 %all-to-all-done.2 = bf16[128,8,640]{2,1,0:T(8,128)(2,1)S(1)} async-done(((bf16[128,8,640]{2,1,0:T(8,128)(2,1)}), bf16[128,8,640]{2,1,0:T(8,128)(2,1)S(1)}, u32[]{:S(2)}, u32[]{:S(2)}) %all-to-all-start.2) | async-done | bytes 1310752 | tf_op jit(solution)/shard_map/all_to_all | solution.py:575
  196.9 0.9 shard_map.118
  197.8 1.2 collective-permute-start.5
  199.0 1.6 copy-done.6
  200.6 1.3 shard_map.119
  201.9 0.1 collective-permute-start.3
  202.0 0.0 collective-permute-done.4.s1
  202.0 0.0 collective-permute-done.5.y1
  202.1 0.0 copy-start.4
  202.1 0.0 copy-start.13
  202.1 0.0 copy-start.15
  202.1 2.7 shard_map.120.before
  204.8 0.0 collective-permute-done.2.x1
  204.8 0.0 collective-permute-done.3.y1
  204.9 5.4 %shard_map.121 = bf16[3072,512]{1,0:T(8,128)(2,1)S(1)} custom-call(bf16[512,2048]{1,0:T(8,128)(2,1)S(1)} %copy-done.4, bf16[512,2048]{1,0:T(8,128)(2,1)} %collective-permute-done.2.x1, bf16[256,2048]{1,0:T(8,128)(2,1)S(1)} %copy-done.1, bf16[256,2048]{1,0:T(8,128)(2,1)} %collective-permute-done.t1, ...), custom_call_target="tpu_custom_call", output_to_operand_aliasing={{}: (8, {})} | custom-call | flops 2147483648 | bytes 10485760 | tf_op jit(solution)/shard_map/pallas_call | solution.py:487
  210.3 44.0 %all_to_all.52.pieces = bf16[64,48,512]{2,1,0:T(8,128)(2,1)S(1)} all-to-all(bf16[64,48,512]{2,1,0:T(8,128)(2,1)S(1)} %bitcast.16), channel_id=1, replica_groups=mesh['y'=4,'x'=4,'z'=4,'core'=2] {'y','x','z'}, dimensions={0} | all-to-all | bytes 6291456 | tf_op jit(solution)/shard_map/all_to_all | solution.py:578
  254.3 1.2 shard_map.122
  255.5 43.5 %all_to_all.53 = bf16[64,48,512]{2,1,0:T(8,128)(2,1)S(1)} all-to-all(bf16[64,48,512]{2,1,0:T(8,128)(2,1)S(1)} %shard_map.122), channel_id=1, replica_groups=mesh['y'=4,'x'=4,'z'=4,'core'=2] {'y','x','z'}, dimensions={0} | all-to-all | bytes 6291456 | tf_op jit(solution)/shard_map/all_to_all | solution.py:578
  299.0 3.4 %collective-permute-start.6 = (bf16[3072,512]{1,0:T(8,128)(2,1)S(1)}, bf16[3072,512]{1,0:T(8,128)(2,1)S(1)}, u32[]{:S(2)}, u32[]{:S(2)}) collective-permute-start(bf16[3072,512]{1,0:T(8,128)(2,1)S(1)} %bitcast.19), channel_id=1, source_target_pairs={{0,1},{1,0},{2,3},{3,2},{4,5},{5,4},{6,7},{7,6},{8,9},{9,8},{10,11... | collective-permute-start | bytes 9437192 | tf_op jit(solution)/shard_map/ppermute | solution.py:572
  302.5 2.8 shard_map.123
  305.3 2.5 collective-permute-done.6.part
  307.8 2.8 shard_map.124
  (20 shorter events, 0.0 us)
Async XLA Ops:
  7.2 117.0 %all-gather.3.cloned.1.call-start = ((), (), s32[]{:S(2)}) async-start(), calls=%async_computation.5 | async-start | bytes 17301504 | tf_op jit(solution)/shard_map/all_gather | solution.py:582
  7.2 1.2 copy-start
  8.4 0.7 copy-start.16
  11.7 41.6 %copy-start.18 = (s32[1,128]{1,0:T(1,128)S(1)}, s32[1,128]{1,0:T(1,128)}, u32[]{:S(2)}) copy-start(s32[1,128]{1,0:T(1,128)} %boundary.1) | copy-start | bytes 1540
  11.7 43.3 %copy-start.1 = (bf16[256,2048]{1,0:T(8,128)(2,1)S(1)}, bf16[256,2048]{1,0:T(8,128)(2,1)}, u32[]{:S(2)}) copy-start(bf16[256,2048]{1,0:T(8,128)(2,1)} %t0.1) | copy-start | bytes 3145732
  11.7 44.7 %copy-start.22 = (s32[1,4,4]{2,1,0:T(4,128)S(1)}, s32[1,4,4]{2,1,0:T(4,128)}, u32[]{:S(2)}) copy-start(s32[1,4,4]{2,1,0:T(4,128)} %param.14) | copy-start | bytes 196
  54.2 0.8 copy-start.5
  55.0 8.8 %collective-permute-start = (bf16[256,2048]{1,0:T(8,128)(2,1)S(1)}, bf16[256,2048]{1,0:T(8,128)(2,1)}, u32[]{:S(2)}, u32[]{:S(2)}) collective-permute-start(bf16[256,2048]{1,0:T(8,128)(2,1)S(1)} %copy-done.1), channel_id=1, source_target_pairs={{0,1},{1,0},{2,3},{3,2},{4,5},{5,4},{6,7},{7,6},{8,9},{9,8},{10,11... | collective-permute-start | bytes 3145736 | tf_op jit(solution)/shard_map/ppermute | solution.py:572
  57.0 2.2 copy-start.2
  61.2 1.3 copy-start.10
  62.5 1.3 copy-start.3
  124.1 38.8 %copy-start.17 = (s32[256,1]{0,1:T(1,128)S(1)}, s32[256,1]{0,1:T(1,128)}, u32[]{:S(2)}) copy-start(s32[256,1]{0,1:T(1,128)} %param.10) | copy-start | bytes 3076
  124.1 38.8 %copy-start.20 = (s32[256,8]{0,1:T(8,128)S(1)}, s32[256,8]{0,1:T(8,128)}, u32[]{:S(2)}) copy-start(s32[256,8]{0,1:T(8,128)} %param.11) | copy-start | bytes 24580
  124.1 38.8 %copy-start.21 = (f32[256,1]{0,1:T(1,128)S(1)}, f32[256,1]{0,1:T(1,128)}, u32[]{:S(2)}) copy-start(f32[256,1]{0,1:T(1,128)} %param.12) | copy-start | bytes 3076
  136.4 26.4 %all-to-all-start.1 = ((bf16[128,8,512]{2,1,0:T(8,128)(2,1)}), bf16[128,8,512]{2,1,0:T(8,128)(2,1)S(1)}, u32[]{:S(2)}, u32[]{:S(2)}) async-start(bf16[128,8,512]{2,1,0:T(8,128)(2,1)} %bitcast.30), calls=%async_computation.1 | async-start | bytes 2097152 | tf_op jit(solution)/shard_map/all_to_all | solution.py:575
  143.7 61.1 %collective-permute-start.2 = (bf16[512,2048]{1,0:T(8,128)(2,1)}, bf16[512,2048]{1,0:T(8,128)(2,1)}, u32[]{:S(2)}, u32[]{:S(2)}) collective-permute-start(bf16[512,2048]{1,0:T(8,128)(2,1)} %get-tuple-element.35.x0), channel_id=1, source_target_pairs={{0,1},{1,0},{2,3},{3,2},{4,5},{5,4},{6,7},{7,6},{8,9},{9,8},{10,11... | collective-permute-start | bytes 6291464 | tf_op jit(solution)/shard_map/ppermute | solution.py:572
  162.9 1.0 copy-start.11
  163.9 32.9 %copy-start.8 = (bf16[512,1024]{1,0:T(8,128)(2,1)S(1)}, bf16[512,1024]{1,0:T(8,128)(2,1)}, u32[]{:S(2)}) copy-start(bf16[512,1024]{1,0:T(8,128)(2,1)} %get-tuple-element.33.slope_factor) | copy-start | bytes 3145732
  167.7 1.1 copy-start.7
  168.8 0.7 copy-start.12
  169.5 0.7 copy-start.19
  170.2 26.7 %all-to-all-start.2 = ((bf16[128,8,640]{2,1,0:T(8,128)(2,1)}), bf16[128,8,640]{2,1,0:T(8,128)(2,1)S(1)}, u32[]{:S(2)}, u32[]{:S(2)}) async-start(bf16[128,8,640]{2,1,0:T(8,128)(2,1)} %bitcast.23), calls=%async_computation.2 | async-start | bytes 2621440 | tf_op jit(solution)/shard_map/all_to_all | solution.py:575
  174.8 27.2 %collective-permute-start.4 = (bf16[512,1024]{1,0:T(8,128)(2,1)}, bf16[512,1024]{1,0:T(8,128)(2,1)}, u32[]{:S(2)}, u32[]{:S(2)}) collective-permute-start(bf16[512,1024]{1,0:T(8,128)(2,1)} %get-tuple-element.42.s0), channel_id=1, source_target_pairs={{0,1},{1,0},{2,3},{3,2},{4,5},{5,4},{6,7},{7,6},{8,9},{9,8},{10,11... | collective-permute-start | bytes 3145736 | tf_op jit(solution)/shard_map/ppermute | solution.py:572
  176.1 2.7 collective-permute-start.1
  178.9 0.7 copy-start.14
  196.9 5.2 %copy-start.9 = (bf16[512,1024]{1,0:T(8,128)(2,1)S(1)}, bf16[512,1024]{1,0:T(8,128)(2,1)}, u32[]{:S(2)}) copy-start(bf16[512,1024]{1,0:T(8,128)(2,1)} %get-tuple-element.42.s0) | copy-start | bytes 3145732
  197.8 4.2 %collective-permute-start.5 = (bf16[512,512]{1,0:T(8,128)(2,1)S(1)}, bf16[512,512]{1,0:T(8,128)(2,1)S(1)}, u32[]{:S(2)}, u32[]{:S(2)}) collective-permute-start(bf16[512,512]{1,0:T(8,128)(2,1)S(1)} %get-tuple-element.44), channel_id=1, source_target_pairs={{0,1},{1,0},{2,3},{3,2},{4,5},{5,4},{6,7},{7,6},{8,9},{9,8},{10,11... | collective-permute-start | bytes 1572872 | tf_op jit(solution)/shard_map/ppermute | solution.py:572
  199.0 1.6 copy-start.6
  201.9 2.9 collective-permute-start.3
  202.1 2.8 copy-start.4
  202.1 2.8 copy-start.13
  202.1 2.8 copy-start.15
  299.0 8.7 %collective-permute-start.6 = (bf16[3072,512]{1,0:T(8,128)(2,1)S(1)}, bf16[3072,512]{1,0:T(8,128)(2,1)S(1)}, u32[]{:S(2)}, u32[]{:S(2)}) collective-permute-start(bf16[3072,512]{1,0:T(8,128)(2,1)S(1)} %bitcast.19), channel_id=1, source_target_pairs={{0,1},{1,0},{2,3},{3,2},{4,5},{5,4},{6,7},{7,6},{8,9},{9,8},{10,11... | collective-permute-start | bytes 9437192 | tf_op jit(solution)/shard_map/ppermute | solution.py:572
Sparse Core Ops, SparseCore 0:
  55.1 68.9 all-gather.2

commit v2 on v1

--- a/solution.py
+++ b/solution.py
@@ -109,28 +109,59 @@
     return ones_where(i == source)
 
 
-def place_kernel(first, second, t_row, sent):
+def place_kernel(text, owner, sent, text_v, t_row, sent_v, sems):
+    steps = 4
+    half = sent.shape[1]
+    piece = half // steps
+    row = pltpu.make_async_copy(owner, t_row, sems.at[0])
+    row.start()
+    loads = []
+    for h in range(2):
+        columns = pl.ds(h * half, half)
+        loads.append(
+            pltpu.make_async_copy(text.at[:, columns], text_v.at[:, columns], sems.at[1 + h])
+        )
+        loads[h].start()
+    row.wait()
     rank_row, _, _ = ranks(t_row[...])
-    sent[...] = spread(t_row[...], rank_row, first[...], second[...], sent.shape[0]).astype(bf16)
+    n = t_row.shape[1]
+    at = iota((sent.shape[0], n), 0)
+    place = jnp.concatenate(
+        [ones_where(at == wide_slot(t_row[...], rank_row, h)) for h in range(2)], axis=1
+    )
+    for load in loads:
+        load.wait()
+    stores = []
+    for i in range(steps):
+        columns = pl.ds(i * piece, piece)
+        both = jnp.concatenate(
+            [text_v[:, pl.ds(h * half + i * piece, piece)] for h in range(2)], axis=0
+        )
+        sent_v[:, columns] = dot(place, both).astype(bf16)
+        stores.append(
+            pltpu.make_async_copy(sent_v.at[:, columns], sent.at[:, columns], sems.at[3 + i])
+        )
+        stores[i].start()
+    for store in stores:
+        store.wait()
 
 
 def place_rows(text, t_row):
     rows, depth = text.shape
-    steps = 4
-    piece = depth // 2 // steps
     return pl.pallas_call(
         place_kernel,
-        grid=(steps,),
-        in_specs=[
-            pl.BlockSpec((rows, piece), lambda i: (0, i)),
-            pl.BlockSpec((rows, piece), lambda i: (0, i + steps)),
-            pl.BlockSpec((1, rows), lambda i: (0, 0)),
+        in_specs=[ANYWHERE, ANYWHERE],
+        out_specs=ANYWHERE,
+        out_shape=jax.ShapeDtypeStruct((4 * rows, depth // 2), bf16),
+        scratch_shapes=[
+            pltpu.VMEM(text.shape, bf16),
+            pltpu.VMEM(t_row.shape, jnp.int32),
+            pltpu.VMEM((4 * rows, depth // 2), bf16),
+            pltpu.SemaphoreType.DMA((7,)),
         ],
-        out_specs=pl.BlockSpec((4 * rows, piece), lambda i: (0, i)),
-        out_shape=jax.ShapeDtypeStruct((4 * rows, depth // 2), bf16),
-        compiler_params=params(),
+        compiler_params=params(58),
         cost_estimate=cost(8 * rows * rows * depth, 3 * 2**20),
-    )(text, text, t_row)
+    )(text, t_row)
 
 
 def embed_kernel(text, w, embed, total):
@@ -306,15 +337,30 @@
 
 
 def loss_kernel(
-    core, back, embed, t_row, negatives, weights, sent_out, text_keep, text_send, sent, both, sems
+    core, back, embed, t_row, negatives, weights, sent_out, text_keep, text_send,
+    back_v, embed_v, sent, both, sems,
 ):
+    parts = 4
+    piece = back.shape[0] // parts
+    rows = [pl.ds(i * piece, piece) for i in range(parts)]
+    load = pltpu.make_async_copy(embed, embed_v, sems.at[parts])
+    loads = [
+        pltpu.make_async_copy(back.at[rows[i], :], back_v.at[rows[i], :], sems.at[i])
+        for i in range(parts)
+    ]
+    for copy in loads:
+        copy.start()
+    load.start()
     rank_row, rank_col, t_col = ranks(t_row[...])
-    buffer = back[...]
+    for copy in loads:
+        copy.wait()
+    buffer = back_v[...]
     first = collect(t_col, rank_col, buffer, 0)
     second = collect(t_col, rank_col, buffer, 1)
     graph = jnp.concatenate([first, second], axis=1)
     graph_b = graph.astype(bf16)
-    text_b = embed[...]
+    load.wait()
+    text_b = embed_v[...]
     text = text_b.astype(f32)
     n = graph.shape[0]
     scale_g = lax.rsqrt(jnp.sum(graph * graph, axis=1, keepdims=True) + norm_floor)
@@ -350,23 +396,30 @@
     both[0] = grad_text[:, :half]
     both[1] = grad_text[:, half:]
     copies = [
-        pltpu.make_async_copy(both.at[core[0]], text_keep, sems.at[0]),
-        pltpu.make_async_copy(both.at[1 - core[0]], text_send, sems.at[1]),
-        pltpu.make_async_copy(sent, sent_out, sems.at[2]),
+        pltpu.make_async_copy(both.at[core[0]], text_keep, sems.at[parts + 1]),
+        pltpu.make_async_copy(both.at[1 - core[0]], text_send, sems.at[parts + 2]),
     ]
-    copies[0].start()
-    copies[1].start()
-    sent[:, :half] = spread(
-        t_row[...], rank_row, grad_b[:, :half], grad_b[:, half:], sent.shape[0]
-    ).astype(bf16)
+    for copy in copies:
+        copy.start()
     shape = (sent.shape[0], sent.shape[1] - half)
     whole = jnp.broadcast_to(total, shape)
     high = whole.astype(bf16).astype(f32)
     mid = (whole - high).astype(bf16).astype(f32)
     lane = jnp.where(iota(shape, 0) % (2 * CAP) == 0, iota(shape, 1), 3)
-    parts = jnp.where(lane == 0, high, jnp.where(lane == 1, mid, whole - high - mid))
-    sent[:, half:] = jnp.where(lane < 3, parts, 0.0).astype(bf16)
-    copies[2].start()
+    value = jnp.where(lane == 0, high, jnp.where(lane == 1, mid, whole - high - mid))
+    sent[:, half:] = jnp.where(lane < 3, value, 0.0).astype(bf16)
+    stacked = jnp.concatenate([grad_b[:, :half], grad_b[:, half:]], axis=0)
+    for i in range(parts):
+        at = iota((piece, n), 0) + i * piece
+        place = jnp.concatenate(
+            [ones_where(at == wide_slot(t_row[...], rank_row, h)) for h in range(2)], axis=1
+        )
+        sent[rows[i], :half] = dot(place, stacked).astype(bf16)
+        copy = pltpu.make_async_copy(
+            sent.at[rows[i], :], sent_out.at[rows[i], :], sems.at[parts + 3 + i]
+        )
+        copy.start()
+        copies.append(copy)
     for copy in copies:
         copy.wait()
 
@@ -376,15 +429,17 @@
     shape = (back.shape[0], back.shape[1] + 128)
     return pl.pallas_call(
         loss_kernel,
-        in_specs=[SMEM] + [VMEM] * 5,
+        in_specs=[SMEM, ANYWHERE, ANYWHERE, VMEM, VMEM, VMEM],
         out_specs=[ANYWHERE] * 3,
         out_shape=[jax.ShapeDtypeStruct(shape, bf16), part, part],
         scratch_shapes=[
+            pltpu.VMEM(back.shape, bf16),
+            pltpu.VMEM(embed.shape, bf16),
             pltpu.VMEM(shape, bf16),
             pltpu.VMEM((2, *part.shape), bf16),
-            pltpu.SemaphoreType.DMA((3,)),
+            pltpu.SemaphoreType.DMA((11,)),
         ],
-        compiler_params=params(),
+        compiler_params=params(58),
         cost_estimate=cost(8 * 2**30, 4 * 2**20),
     )(core, back, embed, t_row, negatives, weights)
 

time: 318 us -> 317 us (level)
  local copies, waits for them, and re-layouts: 12.6 us -> 8.22 us
  Pallas kernels: 40 us -> 43.7 us
    unnamed x46 -> x30, local copies, waits for them, and re-layouts: 12 us -> 7.62 us
    pallas_call x2, Pallas kernels: 6.33 us -> 10.1 us  [the longest x1 6.54 us: loss_side(): pl.pallas_call(loss_kernel, in_specs=[SMEM, ANYWHERE, ANYWHERE, VMEM, VME...]
  transfers between devices with their start and end apart: 10 -> 10, of which waited for: 5 -> 5; matrix products, arithmetic and copies ran while one was open for 0% -> 0% of each run, Pallas kernels for 5% -> 6%
where the time goes in v2:
time: 317 us
  blocking collectives  129 us (41%)
  waiting for transfers between devices  101 us (32%)
  Pallas kernels  43.7 us (14%)
  starting transfers between devices  20.8 us (7%)
  between operations  14.3 us (5%)
  local copies, waits for them, and re-layouts  8.22 us (3%)
    all_to_all x2, blocking collectives, between_chips(): return lax.all_to_all(array, CHIPS, split_axis=0, concat_axis=0, tiled=True)  87.5 us
    all_gather x1, waiting for transfers between devices, body(): extra = lax.all_gather(edges[None], MEMBERS, axis=0, tiled=True)  60.3 us
    all_to_all x1, blocking collectives, redistribute(): return lax.all_to_all(buffer, ALL, split_axis=0, concat_axis=0, tiled=True)  41.8 us
    all_to_all x2, waiting for transfers between devices, redistribute(): return lax.all_to_all(buffer, ALL, split_axis=0, concat_axis=0, tiled=True)  35.2 us
    pallas_call x1, Pallas kernels, forward(): pl.pallas_call(forward_kernel, in_specs=[SMEM, ANYWHERE, ANYWHERE, VMEM,...  12.1 us
    all_to_all x2, starting transfers between devices, redistribute(): return lax.all_to_all(buffer, ALL, split_axis=0, concat_axis=0, tiled=True)  11.9 us
    ppermute x7, starting transfers between devices, swap(): return lax.ppermute(array, 'core', [(0, 1), (1, 0)])  8.81 us
    unnamed x30, local copies, waits for them, and re-layouts  7.62 us
  transfers between devices with their start and end apart: 10, of which 5 were waited for; matrix products, arithmetic and copies ran while one was open for 0% of the time, Pallas kernels for 6%

profile of v2, /device:TPU:1, one launch (start us, length us, event | category | flops | bytes accessed | tf_op | source)
XLA Modules:
  0.0 316.8 jit_solution(2865648257726264724)
XLA Ops:
  7.2 0.0 all-gather.3.cloned.1.call-start
  7.2 0.0 copy-start.12
  7.2 3.6 %shard_map.112 = bf16[1024,1024]{1,0:T(8,128)(2,1)} custom-call(bf16[256,2048]{1,0:T(8,128)(2,1)} %t0.1, s32[1,256]{1,0:T(1,128)} %bitcast.29), custom_call_target="tpu_custom_call" | custom-call | flops 1073741824 | bytes 3145728 | tf_op jit(solution)/shard_map/pallas_call | solution.py:151
  10.8 0.0 copy-start.2
  10.8 0.0 copy-start.14
  10.8 41.8 %all_to_all.51 = bf16[128,8,1024]{2,1,0:T(8,128)(2,1)S(1)} all-to-all(bf16[128,8,1024]{2,1,0:T(8,128)(2,1)} %bitcast.23), channel_id=1, replica_groups=mesh['y'=4,'x'=4,'z'=4,'core'=2] {'y','x','z','core'}, dimensions={0} | all-to-all | bytes 4194304 | tf_op jit(solution)/shard_map/all_to_all | solution.py:630
  52.6 0.0 copy-done.12
  52.6 0.9 shard_map.113
  53.5 0.0 copy-start.4
  53.6 0.8 copy-done.4
  54.3 0.0 all-gather.3.cloned.1.call-update
  54.4 0.0 copy-done.2
  54.4 1.3 collective-permute-start
  55.7 0.0 copy-done.14
  55.7 0.6 reshape.33.index
  56.3 0.0 copy-start
  56.3 2.2 copy-done
  58.5 2.0 shard_map.115.embed
  60.5 0.0 copy-start.8
  60.5 1.3 shard_map.114.local
  61.8 0.0 copy-done.8
  61.8 0.0 copy-start.1
  61.8 1.3 copy-done.1
  63.1 0.0 collective-permute-done.t1
  63.1 60.3 %all-gather.3.cloned.1.call-done = bf16[4096,2048]{1,0:T(8,128)(2,1)} async-done(((bf16[128,2048]{1,0:T(8,128)(2,1)}), bf16[4096,2048]{1,0:T(8,128)(2,1)}) %all-gather.3.cloned.1.call-update) | async-done | bytes 16777232 | tf_op jit(solution)/shard_map/all_gather | solution.py:637
  123.5 12.1 %shard_map.116 = (bf16[512,2048]{1,0:T(8,128)(2,1)}, bf16[512,1024]{1,0:T(8,128)(2,1)}, bf16[512,1024]{1,0:T(8,128)(2,1)}, bf16[1024,512]{1,0:T(8,128)(2,1)}) custom-call(s32[1,16]{1,0:T(1,128)} %reshape.33.index, bf16[32,128,2048]{2,1,0:T(8,128)(2,1)} %bitcast.22, bf16[4,128,2048]{2,1,0:T(8,128)(2,1)} %copy-done.1, bf16[4,4,128,128]{3,2,1,0:T(8,128)(2,1)} %bitcast.27, ...), custom_call_target="tpu_custom_call" | custom-call | flops 3221225472 | bytes 23068672 | tf_op jit(solution)/shard_map/pallas_call | solution.py:321
  135.6 7.3 %all-to-all-start.1 = ((bf16[128,8,512]{2,1,0:T(8,128)(2,1)}), bf16[128,8,512]{2,1,0:T(8,128)(2,1)S(1)}, u32[]{:S(2)}, u32[]{:S(2)}) async-start(bf16[128,8,512]{2,1,0:T(8,128)(2,1)} %bitcast.26), calls=%async_computation.1 | async-start | bytes 2097152 | tf_op jit(solution)/shard_map/all_to_all | solution.py:630
  142.9 1.3 collective-permute-start.2
  144.2 17.8 %all-to-all-done.1 = bf16[128,8,512]{2,1,0:T(8,128)(2,1)S(1)} async-done(((bf16[128,8,512]{2,1,0:T(8,128)(2,1)}), bf16[128,8,512]{2,1,0:T(8,128)(2,1)S(1)}, u32[]{:S(2)}, u32[]{:S(2)}) %all-to-all-start.1) | async-done | bytes 1048608 | tf_op jit(solution)/shard_map/all_to_all | solution.py:630
  162.0 0.0 copy-start.13
  162.0 1.0 copy-done.13
  163.0 6.5 %shard_map.117 = (bf16[1024,640]{1,0:T(8,128)(2,1)}, bf16[256,512]{1,0:T(8,128)(2,1)}, bf16[256,512]{1,0:T(8,128)(2,1)}) custom-call(s32[1]{0:T(128)} %bitcast.core.member, bf16[1024,512]{1,0:T(8,128)(2,1)} %bitcast.25, bf16[256,1024]{1,0:T(8,128)(2,1)} %copy-done.8, s32[1,256]{1,0:T(1,128)} %bitcast.30, s32[8,256]{1,0:T(8,128)} %bitcast.28, f32[1,256]{1,0:T(1,128)} %bitcast.31), custom_call_target="tpu_custom_call" | custom-call | flops 8589934592 | bytes 4194304 | tf_op jit(solution)/shard_map/pallas_call | solution.py:430
  169.6 4.6 %all-to-all-start.2 = ((bf16[128,8,640]{2,1,0:T(8,128)(2,1)}), bf16[128,8,640]{2,1,0:T(8,128)(2,1)S(1)}, u32[]{:S(2)}, u32[]{:S(2)}) async-start(bf16[128,8,640]{2,1,0:T(8,128)(2,1)} %bitcast.24), calls=%async_computation.2 | async-start | bytes 2621440 | tf_op jit(solution)/shard_map/all_to_all | solution.py:630
  174.2 1.3 collective-permute-start.4
  175.5 0.1 collective-permute-start.1
  175.6 2.6 collective-permute-done.1.g1
  178.3 0.7 copy-done.10
  179.0 17.3 %all-to-all-done.2 = bf16[128,8,640]{2,1,0:T(8,128)(2,1)S(1)} async-done(((bf16[128,8,640]{2,1,0:T(8,128)(2,1)}), bf16[128,8,640]{2,1,0:T(8,128)(2,1)S(1)}, u32[]{:S(2)}, u32[]{:S(2)}) %all-to-all-start.2) | async-done | bytes 1310752 | tf_op jit(solution)/shard_map/all_to_all | solution.py:630
  196.3 0.0 copy-done.6
  196.3 0.9 shard_map.118
  197.2 1.2 collective-permute-start.5
  198.5 1.6 copy-done.5
  200.0 1.3 shard_map.119
  201.3 0.1 collective-permute-start.3
  201.4 0.0 collective-permute-done.4.s1
  201.4 0.0 collective-permute-done.5.y1
  201.4 0.0 copy-done.7
  201.5 0.0 copy-start.3
  201.5 0.0 copy-start.9
  201.5 0.0 copy-start.11
  201.5 2.7 shard_map.120.before
  204.2 0.0 collective-permute-done.2.x1
  204.2 0.0 collective-permute-done.3.y1
  204.3 0.0 copy-done.3
  204.3 0.0 copy-done.9
  204.3 0.0 copy-done.11
  204.3 5.4 %shard_map.121 = bf16[3072,512]{1,0:T(8,128)(2,1)S(1)} custom-call(bf16[512,2048]{1,0:T(8,128)(2,1)S(1)} %copy-done.3, bf16[512,2048]{1,0:T(8,128)(2,1)} %collective-permute-done.2.x1, bf16[256,2048]{1,0:T(8,128)(2,1)S(1)} %copy-done.2, bf16[256,2048]{1,0:T(8,128)(2,1)} %collective-permute-done.t1, ...), custom_call_target="tpu_custom_call", output_to_operand_aliasing={{}: (8, {})} | custom-call | flops 2147483648 | bytes 10485760 | tf_op jit(solution)/shard_map/pallas_call | solution.py:542
  209.7 44.0 %all_to_all.52.pieces = bf16[64,48,512]{2,1,0:T(8,128)(2,1)S(1)} all-to-all(bf16[64,48,512]{2,1,0:T(8,128)(2,1)S(1)} %bitcast.16), channel_id=1, replica_groups=mesh['y'=4,'x'=4,'z'=4,'core'=2] {'y','x','z'}, dimensions={0} | all-to-all | bytes 6291456 | tf_op jit(solution)/shard_map/all_to_all | solution.py:633
  253.7 1.2 shard_map.122
  254.9 43.5 %all_to_all.53 = bf16[64,48,512]{2,1,0:T(8,128)(2,1)S(1)} all-to-all(bf16[64,48,512]{2,1,0:T(8,128)(2,1)S(1)} %shard_map.122), channel_id=1, replica_groups=mesh['y'=4,'x'=4,'z'=4,'core'=2] {'y','x','z'}, dimensions={0} | all-to-all | bytes 6291456 | tf_op jit(solution)/shard_map/all_to_all | solution.py:633
  298.4 3.4 %collective-permute-start.6 = (bf16[3072,512]{1,0:T(8,128)(2,1)S(1)}, bf16[3072,512]{1,0:T(8,128)(2,1)S(1)}, u32[]{:S(2)}, u32[]{:S(2)}) collective-permute-start(bf16[3072,512]{1,0:T(8,128)(2,1)S(1)} %bitcast.19), channel_id=1, source_target_pairs={{0,1},{1,0},{2,3},{3,2},{4,5},{5,4},{6,7},{7,6},{8,9},{9,8},{10,11... | collective-permute-start | bytes 9437192 | tf_op jit(solution)/shard_map/ppermute | solution.py:627
  301.9 2.8 shard_map.123
  304.7 2.5 collective-permute-done.6.part
  307.2 2.8 shard_map.124
  (4 shorter events, 0.0 us)
Async XLA Ops:
  7.2 116.3 %all-gather.3.cloned.1.call-start = ((), (), s32[]{:S(2)}) async-start(), calls=%async_computation.5 | async-start | bytes 17301504 | tf_op jit(solution)/shard_map/all_gather | solution.py:637
  7.2 45.4 %copy-start.12 = (s32[1,128]{1,0:T(1,128)S(1)}, s32[1,128]{1,0:T(1,128)}, u32[]{:S(2)}) copy-start(s32[1,128]{1,0:T(1,128)} %boundary.1) | copy-start | bytes 1540
  10.8 43.5 %copy-start.2 = (bf16[256,2048]{1,0:T(8,128)(2,1)S(1)}, bf16[256,2048]{1,0:T(8,128)(2,1)}, u32[]{:S(2)}) copy-start(bf16[256,2048]{1,0:T(8,128)(2,1)} %t0.1) | copy-start | bytes 3145732
  10.8 44.9 %copy-start.14 = (s32[1,4,4]{2,1,0:T(4,128)S(1)}, s32[1,4,4]{2,1,0:T(4,128)}, u32[]{:S(2)}) copy-start(s32[1,4,4]{2,1,0:T(4,128)} %param.14) | copy-start | bytes 196
  53.5 0.8 copy-start.4
  54.4 8.8 %collective-permute-start = (bf16[256,2048]{1,0:T(8,128)(2,1)S(1)}, bf16[256,2048]{1,0:T(8,128)(2,1)}, u32[]{:S(2)}, u32[]{:S(2)}) collective-permute-start(bf16[256,2048]{1,0:T(8,128)(2,1)S(1)} %copy-done.2), channel_id=1, source_target_pairs={{0,1},{1,0},{2,3},{3,2},{4,5},{5,4},{6,7},{7,6},{8,9},{9,8},{10,11... | collective-permute-start | bytes 3145736 | tf_op jit(solution)/shard_map/ppermute | solution.py:627
  56.3 2.2 copy-start
  60.5 1.3 copy-start.8
  61.8 1.3 copy-start.1
  135.6 26.4 %all-to-all-start.1 = ((bf16[128,8,512]{2,1,0:T(8,128)(2,1)}), bf16[128,8,512]{2,1,0:T(8,128)(2,1)S(1)}, u32[]{:S(2)}, u32[]{:S(2)}) async-start(bf16[128,8,512]{2,1,0:T(8,128)(2,1)} %bitcast.26), calls=%async_computation.1 | async-start | bytes 2097152 | tf_op jit(solution)/shard_map/all_to_all | solution.py:630
  142.9 61.4 %collective-permute-start.2 = (bf16[512,2048]{1,0:T(8,128)(2,1)}, bf16[512,2048]{1,0:T(8,128)(2,1)}, u32[]{:S(2)}, u32[]{:S(2)}) collective-permute-start(bf16[512,2048]{1,0:T(8,128)(2,1)} %get-tuple-element.35.x0), channel_id=1, source_target_pairs={{0,1},{1,0},{2,3},{3,2},{4,5},{5,4},{6,7},{7,6},{8,9},{9,8},{10,11... | collective-permute-start | bytes 6291464 | tf_op jit(solution)/shard_map/ppermute | solution.py:627
  162.0 1.0 copy-start.13
  163.0 33.3 %copy-start.6 = (bf16[512,1024]{1,0:T(8,128)(2,1)S(1)}, bf16[512,1024]{1,0:T(8,128)(2,1)}, u32[]{:S(2)}) copy-start(bf16[512,1024]{1,0:T(8,128)(2,1)} %get-tuple-element.33.slope_factor) | copy-start | bytes 3145732
  169.6 26.7 %all-to-all-start.2 = ((bf16[128,8,640]{2,1,0:T(8,128)(2,1)}), bf16[128,8,640]{2,1,0:T(8,128)(2,1)S(1)}, u32[]{:S(2)}, u32[]{:S(2)}) async-start(bf16[128,8,640]{2,1,0:T(8,128)(2,1)} %bitcast.24), calls=%async_computation.2 | async-start | bytes 2621440 | tf_op jit(solution)/shard_map/all_to_all | solution.py:630
  174.2 27.2 %collective-permute-start.4 = (bf16[512,1024]{1,0:T(8,128)(2,1)}, bf16[512,1024]{1,0:T(8,128)(2,1)}, u32[]{:S(2)}, u32[]{:S(2)}) collective-permute-start(bf16[512,1024]{1,0:T(8,128)(2,1)} %get-tuple-element.42.s0), channel_id=1, source_target_pairs={{0,1},{1,0},{2,3},{3,2},{4,5},{5,4},{6,7},{7,6},{8,9},{9,8},{10,11... | collective-permute-start | bytes 3145736 | tf_op jit(solution)/shard_map/ppermute | solution.py:627
  175.5 2.7 collective-permute-start.1
  178.3 0.7 copy-start.10
  196.3 5.2 %copy-start.7 = (bf16[512,1024]{1,0:T(8,128)(2,1)S(1)}, bf16[512,1024]{1,0:T(8,128)(2,1)}, u32[]{:S(2)}) copy-start(bf16[512,1024]{1,0:T(8,128)(2,1)} %get-tuple-element.42.s0) | copy-start | bytes 3145732
  197.2 4.2 %collective-permute-start.5 = (bf16[512,512]{1,0:T(8,128)(2,1)S(1)}, bf16[512,512]{1,0:T(8,128)(2,1)S(1)}, u32[]{:S(2)}, u32[]{:S(2)}) collective-permute-start(bf16[512,512]{1,0:T(8,128)(2,1)S(1)} %get-tuple-element.44), channel_id=1, source_target_pairs={{0,1},{1,0},{2,3},{3,2},{4,5},{5,4},{6,7},{7,6},{8,9},{9,8},{10,11... | collective-permute-start | bytes 1572872 | tf_op jit(solution)/shard_map/ppermute | solution.py:627
  198.4 1.6 copy-start.5
  201.3 2.9 collective-permute-start.3
  201.5 2.8 copy-start.3
  201.5 2.8 copy-start.9
  201.5 2.8 copy-start.11
  298.4 8.7 %collective-permute-start.6 = (bf16[3072,512]{1,0:T(8,128)(2,1)S(1)}, bf16[3072,512]{1,0:T(8,128)(2,1)S(1)}, u32[]{:S(2)}, u32[]{:S(2)}) collective-permute-start(bf16[3072,512]{1,0:T(8,128)(2,1)S(1)} %bitcast.19), channel_id=1, source_target_pairs={{0,1},{1,0},{2,3},{3,2},{4,5},{5,4},{6,7},{7,6},{8,9},{9,8},{10,11... | collective-permute-start | bytes 9437192 | tf_op jit(solution)/shard_map/ppermute | solution.py:627
Sparse Core Ops, SparseCore 0:
  54.5 68.9 all-gather.2

commit v3 on v2

--- a/solution.py
+++ b/solution.py
@@ -276,13 +276,12 @@
         copy.start()
         stores.append(copy)
 
-    count = BLOCKS * PICKS
-    for n in range(count // 2):
-        start(n)
-    load_proj.start()
-    load_gnn.start()
-    for n in range(count // 2, count):
-        start(n)
+    def start_block(b):
+        for p in range(PICKS):
+            start(b * PICKS + p)
+
+    start_block(0)
+    start_block(1)
     order = weave(tile)
     for pair in range(BLOCKS // 2):
         rows = pl.ds(2 * pair * tile, 2 * tile)
@@ -290,6 +289,12 @@
             for p in range(PICKS):
                 n = b * PICKS + p
                 pltpu.make_async_copy(extra.at[0], place(n), sems.at[n]).wait()
+            if b == 0:
+                load_proj.start()
+            if b == 1:
+                load_gnn.start()
+                start_block(2)
+                start_block(3)
             weights = jnp.concatenate([adj[b, p] for p in range(PICKS)], axis=1)
             texts_v[pl.ds(b * tile, tile), :] = dot(weights, src[b]).astype(bf16)
         store(texts_v, texts, rows)
@@ -444,7 +449,14 @@
     )(core, back, embed, t_row, negatives, weights)
 
 
-def slope_kernel(loss_scale, core, back, slope_factor, slope, keep, send, loss):
+def slope_kernel(
+    loss_scale, core, back, slope_factor, w, slope, keep, send, loss, w_near, sems
+):
+    loads = []
+    for i in range(2):
+        part = pl.ds(i * (w.shape[0] // 2), w.shape[0] // 2)
+        loads.append(pltpu.make_async_copy(w.at[part, :], w_near.at[part, :], sems.at[i]))
+        loads[i].start()
     k = core[0]
     half = keep.shape[1]
     tile = slope.shape[0] // BLOCKS
@@ -459,24 +471,28 @@
     loss[...] = jnp.broadcast_to(
         jnp.sum(back[:, half:].astype(f32), keepdims=True) * loss_scale, loss.shape
     )
-
-
-def slopes(core, back, slope_factor, loss_scale):
+    for load in loads:
+        load.wait()
+
+
+def slopes(core, back, slope_factor, w, loss_scale):
     slots, width = slope_factor.shape
     part = jax.ShapeDtypeStruct((slots, width // 2), bf16)
     return pl.pallas_call(
         functools.partial(slope_kernel, loss_scale),
-        in_specs=[SMEM] + [VMEM] * 2,
-        out_specs=[VMEM] * 4,
+        in_specs=[SMEM] + [VMEM] * 2 + [ANYWHERE],
+        out_specs=[VMEM] * 5,
         out_shape=[
             jax.ShapeDtypeStruct((slots, width), bf16),
             part,
             part,
             jax.ShapeDtypeStruct((1, 128), f32),
+            jax.ShapeDtypeStruct(w.shape, bf16),
         ],
+        scratch_shapes=[pltpu.SemaphoreType.DMA((2,))],
         compiler_params=params(),
         cost_estimate=cost(2 * slots * slots * width, 4 * 2**20),
-    )(core, back, slope_factor)
+    )(core, back, slope_factor, w)
 
 
 def grad_sum_kernel(core, slope, w, keep, send):
@@ -646,11 +662,11 @@
     )
     text_got = swap(text_send)
     back, text_got = together((redistribute(sent), text_got))
-    slope, slope_keep, slope_send, loss = slopes(
-        core, back, slope_factor, 1.0 / (owners * rows)
+    slope, slope_keep, slope_send, loss, w_near = slopes(
+        core, back, slope_factor, w_gnn, 1.0 / (owners * rows)
     )
     slope_got = swap(slope_send)
-    keep, send = grad_sums(core, slope, w_gnn)
+    keep, send = grad_sums(core, slope, w_near)
     total = layer_weights((summed, other_summed), (slope_keep, slope_got), text.shape[1])
     total = proj_weights(
         (texts, other_texts), (text, other_text), (keep, swap(send)), (text_keep, text_got), total

time: 317 us -> 318 us (level)
    unnamed x30 -> x32, local copies, waits for them, and re-layouts: 7.62 us -> 7.24 us
  transfers between devices with their start and end apart: 10 -> 10, of which waited for: 5 -> 6; matrix products, arithmetic and copies ran while one was open for 0% -> 0% of each run, Pallas kernels for 6% -> 6%
where the time goes in v3:
time: 318 us; the launch traced here: 317 us
  blocking collectives  129 us (41%)
  waiting for transfers between devices  101 us (32%)
  Pallas kernels  43.8 us (14%)
  starting transfers between devices  21.3 us (7%)
  between operations  14.3 us (4%)
  local copies, waits for them, and re-layouts  7.84 us (2%)
    all_to_all x2, blocking collectives, between_chips(): return lax.all_to_all(array, CHIPS, split_axis=0, concat_axis=0, tiled=True)  87.5 us
    all_gather x1, waiting for transfers between devices, body(): extra = lax.all_gather(edges[None], MEMBERS, axis=0, tiled=True)  60.3 us
    all_to_all x1, blocking collectives, redistribute(): return lax.all_to_all(buffer, ALL, split_axis=0, concat_axis=0, tiled=True)  41.8 us
    all_to_all x2, waiting for transfers between devices, redistribute(): return lax.all_to_all(buffer, ALL, split_axis=0, concat_axis=0, tiled=True)  35.2 us
    all_to_all x2, starting transfers between devices, redistribute(): return lax.all_to_all(buffer, ALL, split_axis=0, concat_axis=0, tiled=True)  12.4 us
    pallas_call x1, Pallas kernels, forward(): pl.pallas_call(forward_kernel, in_specs=[SMEM, ANYWHERE, ANYWHERE, VMEM,...  12.1 us
    ppermute x7, starting transfers between devices, swap(): return lax.ppermute(array, 'core', [(0, 1), (1, 0)])  8.91 us
    unnamed x32, local copies, waits for them, and re-layouts  7.24 us
  transfers between devices with their start and end apart: 10, of which 6 were waited for; matrix products, arithmetic and copies ran while one was open for 0% of the time, Pallas kernels for 6%

profile of v3, /device:TPU:1, one launch (start us, length us, event | category | flops | bytes accessed | tf_op | source)
XLA Modules:
  0.0 317.3 jit_solution(15182595008164903456)
XLA Ops:
  7.2 0.0 all-gather.3.cloned.1.call-start
  7.2 0.0 copy-start.13
  7.2 3.6 %shard_map.112 = bf16[1024,1024]{1,0:T(8,128)(2,1)} custom-call(bf16[256,2048]{1,0:T(8,128)(2,1)} %t0.1, s32[1,256]{1,0:T(1,128)} %bitcast.29), custom_call_target="tpu_custom_call" | custom-call | flops 1073741824 | bytes 3145728 | tf_op jit(solution)/shard_map/pallas_call | solution.py:151
  10.8 0.0 copy-start.3
  10.8 0.0 copy-start.15
  10.8 41.8 %all_to_all.51 = bf16[128,8,1024]{2,1,0:T(8,128)(2,1)S(1)} all-to-all(bf16[128,8,1024]{2,1,0:T(8,128)(2,1)} %bitcast.23), channel_id=1, replica_groups=mesh['y'=4,'x'=4,'z'=4,'core'=2] {'y','x','z','core'}, dimensions={0} | all-to-all | bytes 4194304 | tf_op jit(solution)/shard_map/all_to_all | solution.py:646
  52.6 0.0 copy-done.13
  52.6 0.9 shard_map.113
  53.5 0.0 copy-start.6
  53.6 0.8 copy-done.6
  54.3 0.0 all-gather.3.cloned.1.call-update
  54.4 0.0 copy-done.3
  54.4 1.3 collective-permute-start
  55.7 0.0 copy-done.15
  55.7 0.6 reshape.33.index
  56.3 0.0 copy-start
  56.3 2.2 copy-done
  58.5 2.0 shard_map.115.embed
  60.5 0.0 copy-start.9
  60.5 1.3 shard_map.114.local
  61.8 0.0 copy-done.9
  61.8 0.0 copy-start.2
  61.8 1.3 copy-done.2
  63.1 0.0 collective-permute-done.t1
  63.1 60.3 %all-gather.3.cloned.1.call-done = bf16[4096,2048]{1,0:T(8,128)(2,1)} async-done(((bf16[128,2048]{1,0:T(8,128)(2,1)}), bf16[4096,2048]{1,0:T(8,128)(2,1)}) %all-gather.3.cloned.1.call-update) | async-done | bytes 16777232 | tf_op jit(solution)/shard_map/all_gather | solution.py:653
  123.5 12.1 %shard_map.116 = (bf16[512,2048]{1,0:T(8,128)(2,1)}, bf16[512,1024]{1,0:T(8,128)(2,1)}, bf16[512,1024]{1,0:T(8,128)(2,1)}, bf16[1024,512]{1,0:T(8,128)(2,1)}) custom-call(s32[1,16]{1,0:T(1,128)} %reshape.33.index, bf16[32,128,2048]{2,1,0:T(8,128)(2,1)} %bitcast.22, bf16[4,128,2048]{2,1,0:T(8,128)(2,1)} %copy-done.2, bf16[4,4,128,128]{3,2,1,0:T(8,128)(2,1)} %bitcast.27, ...), custom_call_target="tpu_custom_call" | custom-call | flops 3221225472 | bytes 23068672 | tf_op jit(solution)/shard_map/pallas_call | solution.py:326
  135.6 7.6 %all-to-all-start.1 = ((bf16[128,8,512]{2,1,0:T(8,128)(2,1)}), bf16[128,8,512]{2,1,0:T(8,128)(2,1)S(1)}, u32[]{:S(2)}, u32[]{:S(2)}) async-start(bf16[128,8,512]{2,1,0:T(8,128)(2,1)} %bitcast.26), calls=%async_computation.1 | async-start | bytes 2097152 | tf_op jit(solution)/shard_map/all_to_all | solution.py:646
  143.2 1.3 collective-permute-start.2
  144.5 17.8 %all-to-all-done.1 = bf16[128,8,512]{2,1,0:T(8,128)(2,1)S(1)} async-done(((bf16[128,8,512]{2,1,0:T(8,128)(2,1)}), bf16[128,8,512]{2,1,0:T(8,128)(2,1)S(1)}, u32[]{:S(2)}, u32[]{:S(2)}) %all-to-all-start.1) | async-done | bytes 1048608 | tf_op jit(solution)/shard_map/all_to_all | solution.py:646
  162.3 0.0 copy-start.14
  162.3 1.0 copy-done.14
  163.3 6.5 %shard_map.117 = (bf16[1024,640]{1,0:T(8,128)(2,1)}, bf16[256,512]{1,0:T(8,128)(2,1)}, bf16[256,512]{1,0:T(8,128)(2,1)}) custom-call(s32[1]{0:T(128)} %bitcast.core.member, bf16[1024,512]{1,0:T(8,128)(2,1)} %bitcast.25, bf16[256,1024]{1,0:T(8,128)(2,1)} %copy-done.9, s32[1,256]{1,0:T(1,128)} %bitcast.30, s32[8,256]{1,0:T(8,128)} %bitcast.28, f32[1,256]{1,0:T(1,128)} %bitcast.31), custom_call_target="tpu_custom_call" | custom-call | flops 8589934592 | bytes 4194304 | tf_op jit(solution)/shard_map/pallas_call | solution.py:435
  169.8 0.0 copy-start.1
  169.8 4.8 %all-to-all-start.2 = ((bf16[128,8,640]{2,1,0:T(8,128)(2,1)}), bf16[128,8,640]{2,1,0:T(8,128)(2,1)S(1)}, u32[]{:S(2)}, u32[]{:S(2)}) async-start(bf16[128,8,640]{2,1,0:T(8,128)(2,1)} %bitcast.24), calls=%async_computation.2 | async-start | bytes 2621440 | tf_op jit(solution)/shard_map/all_to_all | solution.py:646
  174.6 1.3 collective-permute-start.4
  175.9 0.1 collective-permute-start.1
  176.0 2.6 collective-permute-done.1.g1
  178.6 0.7 copy-done.11
  179.3 17.3 %all-to-all-done.2 = bf16[128,8,640]{2,1,0:T(8,128)(2,1)S(1)} async-done(((bf16[128,8,640]{2,1,0:T(8,128)(2,1)}), bf16[128,8,640]{2,1,0:T(8,128)(2,1)S(1)}, u32[]{:S(2)}, u32[]{:S(2)}) %all-to-all-start.2) | async-done | bytes 1310752 | tf_op jit(solution)/shard_map/all_to_all | solution.py:646
  196.6 0.0 copy-done.1
  196.6 1.2 copy-done.7
  197.9 1.2 shard_map.118
  199.1 1.3 collective-permute-start.5
  200.4 1.3 shard_map.119
  201.7 0.1 collective-permute-start.3
  201.8 0.0 collective-permute-done.4.s1
  201.8 0.1 collective-permute-done.5.y1
  201.9 0.0 copy-done.8
  201.9 0.0 copy-start.12
  201.9 2.7 shard_map.120.before
  204.7 0.0 collective-permute-done.2.x1
  204.7 0.0 collective-permute-done.3.y1
  204.7 0.0 copy-done.4
  204.7 0.0 copy-done.5
  204.7 0.0 copy-done.10
  204.7 0.0 copy-done.12
  204.7 5.4 %shard_map.121 = bf16[3072,512]{1,0:T(8,128)(2,1)S(1)} custom-call(bf16[512,2048]{1,0:T(8,128)(2,1)S(1)} %copy-done.5, bf16[512,2048]{1,0:T(8,128)(2,1)} %collective-permute-done.2.x1, bf16[256,2048]{1,0:T(8,128)(2,1)S(1)} %copy-done.4, bf16[256,2048]{1,0:T(8,128)(2,1)} %collective-permute-done.t1, ...), custom_call_target="tpu_custom_call", output_to_operand_aliasing={{}: (8, {})} | custom-call | flops 2147483648 | bytes 10485760 | tf_op jit(solution)/shard_map/pallas_call | solution.py:558
  210.2 44.0 %all_to_all.52.pieces = bf16[64,48,512]{2,1,0:T(8,128)(2,1)S(1)} all-to-all(bf16[64,48,512]{2,1,0:T(8,128)(2,1)S(1)} %bitcast.16), channel_id=1, replica_groups=mesh['y'=4,'x'=4,'z'=4,'core'=2] {'y','x','z'}, dimensions={0} | all-to-all | bytes 6291456 | tf_op jit(solution)/shard_map/all_to_all | solution.py:649
  254.2 1.2 shard_map.122
  255.4 43.4 %all_to_all.53 = bf16[64,48,512]{2,1,0:T(8,128)(2,1)S(1)} all-to-all(bf16[64,48,512]{2,1,0:T(8,128)(2,1)S(1)} %shard_map.122), channel_id=1, replica_groups=mesh['y'=4,'x'=4,'z'=4,'core'=2] {'y','x','z'}, dimensions={0} | all-to-all | bytes 6291456 | tf_op jit(solution)/shard_map/all_to_all | solution.py:649
  298.9 3.5 %collective-permute-start.6 = (bf16[3072,512]{1,0:T(8,128)(2,1)S(1)}, bf16[3072,512]{1,0:T(8,128)(2,1)S(1)}, u32[]{:S(2)}, u32[]{:S(2)}) collective-permute-start(bf16[3072,512]{1,0:T(8,128)(2,1)S(1)} %bitcast.19), channel_id=1, source_target_pairs={{0,1},{1,0},{2,3},{3,2},{4,5},{5,4},{6,7},{7,6},{8,9},{9,8},{10,11... | collective-permute-start | bytes 9437192 | tf_op jit(solution)/shard_map/ppermute | solution.py:643
  302.3 2.8 shard_map.123
  305.1 2.5 collective-permute-done.6.part
  307.6 2.8 shard_map.124
  (6 shorter events, 0.0 us)
Async XLA Ops:
  7.2 116.3 %all-gather.3.cloned.1.call-start = ((), (), s32[]{:S(2)}) async-start(), calls=%async_computation.5 | async-start | bytes 17301504 | tf_op jit(solution)/shard_map/all_gather | solution.py:653
  7.2 45.4 %copy-start.13 = (s32[1,128]{1,0:T(1,128)S(1)}, s32[1,128]{1,0:T(1,128)}, u32[]{:S(2)}) copy-start(s32[1,128]{1,0:T(1,128)} %boundary.1) | copy-start | bytes 1540
  10.8 43.5 %copy-start.3 = (bf16[256,2048]{1,0:T(8,128)(2,1)S(1)}, bf16[256,2048]{1,0:T(8,128)(2,1)}, u32[]{:S(2)}) copy-start(bf16[256,2048]{1,0:T(8,128)(2,1)} %t0.1) | copy-start | bytes 3145732
  10.8 44.9 %copy-start.15 = (s32[1,4,4]{2,1,0:T(4,128)S(1)}, s32[1,4,4]{2,1,0:T(4,128)}, u32[]{:S(2)}) copy-start(s32[1,4,4]{2,1,0:T(4,128)} %param.14) | copy-start | bytes 196
  53.5 0.8 copy-start.6
  54.4 8.8 %collective-permute-start = (bf16[256,2048]{1,0:T(8,128)(2,1)S(1)}, bf16[256,2048]{1,0:T(8,128)(2,1)}, u32[]{:S(2)}, u32[]{:S(2)}) collective-permute-start(bf16[256,2048]{1,0:T(8,128)(2,1)S(1)} %copy-done.3), channel_id=1, source_target_pairs={{0,1},{1,0},{2,3},{3,2},{4,5},{5,4},{6,7},{7,6},{8,9},{9,8},{10,11... | collective-permute-start | bytes 3145736 | tf_op jit(solution)/shard_map/ppermute | solution.py:643
  56.3 2.2 copy-start
  60.5 1.3 copy-start.9
  61.8 1.3 copy-start.2
  135.6 26.8 %all-to-all-start.1 = ((bf16[128,8,512]{2,1,0:T(8,128)(2,1)}), bf16[128,8,512]{2,1,0:T(8,128)(2,1)S(1)}, u32[]{:S(2)}, u32[]{:S(2)}) async-start(bf16[128,8,512]{2,1,0:T(8,128)(2,1)} %bitcast.26), calls=%async_computation.1 | async-start | bytes 2097152 | tf_op jit(solution)/shard_map/all_to_all | solution.py:646
  143.2 61.5 %collective-permute-start.2 = (bf16[512,2048]{1,0:T(8,128)(2,1)}, bf16[512,2048]{1,0:T(8,128)(2,1)}, u32[]{:S(2)}, u32[]{:S(2)}) collective-permute-start(bf16[512,2048]{1,0:T(8,128)(2,1)} %get-tuple-element.36.x0), channel_id=1, source_target_pairs={{0,1},{1,0},{2,3},{3,2},{4,5},{5,4},{6,7},{7,6},{8,9},{9,8},{10,11... | collective-permute-start | bytes 6291464 | tf_op jit(solution)/shard_map/ppermute | solution.py:643
  162.3 1.0 copy-start.14
  169.8 26.8 %copy-start.1 = (bf16[1024,1024]{1,0:T(8,128)(2,1)S(1)}, bf16[1024,1024]{1,0:T(8,128)(2,1)}, u32[]{:S(2)}) copy-start(bf16[1024,1024]{1,0:T(8,128)(2,1)} %w.3) | copy-start | bytes 6291460
  169.8 26.8 %all-to-all-start.2 = ((bf16[128,8,640]{2,1,0:T(8,128)(2,1)}), bf16[128,8,640]{2,1,0:T(8,128)(2,1)S(1)}, u32[]{:S(2)}, u32[]{:S(2)}) async-start(bf16[128,8,640]{2,1,0:T(8,128)(2,1)} %bitcast.24), calls=%async_computation.2 | async-start | bytes 2621440 | tf_op jit(solution)/shard_map/all_to_all | solution.py:646
  174.6 27.2 %collective-permute-start.4 = (bf16[512,1024]{1,0:T(8,128)(2,1)}, bf16[512,1024]{1,0:T(8,128)(2,1)}, u32[]{:S(2)}, u32[]{:S(2)}) collective-permute-start(bf16[512,1024]{1,0:T(8,128)(2,1)} %get-tuple-element.44.s0), channel_id=1, source_target_pairs={{0,1},{1,0},{2,3},{3,2},{4,5},{5,4},{6,7},{7,6},{8,9},{9,8},{10,11... | collective-permute-start | bytes 3145736 | tf_op jit(solution)/shard_map/ppermute | solution.py:643
  175.9 2.7 collective-permute-start.1
  178.6 0.7 copy-start.11
  196.6 1.2 copy-start.7
  197.9 4.0 %copy-start.8 = (bf16[512,1024]{1,0:T(8,128)(2,1)S(1)}, bf16[512,1024]{1,0:T(8,128)(2,1)}, u32[]{:S(2)}) copy-start(bf16[512,1024]{1,0:T(8,128)(2,1)} %get-tuple-element.44.s0) | copy-start | bytes 3145732
  199.1 2.8 collective-permute-start.5
  201.7 3.0 collective-permute-start.3
  201.9 2.8 copy-start.4
  201.9 2.8 copy-start.5
  201.9 2.8 copy-start.10
  201.9 2.8 copy-start.12
  298.9 8.7 %collective-permute-start.6 = (bf16[3072,512]{1,0:T(8,128)(2,1)S(1)}, bf16[3072,512]{1,0:T(8,128)(2,1)S(1)}, u32[]{:S(2)}, u32[]{:S(2)}) collective-permute-start(bf16[3072,512]{1,0:T(8,128)(2,1)S(1)} %bitcast.19), channel_id=1, source_target_pairs={{0,1},{1,0},{2,3},{3,2},{4,5},{5,4},{6,7},{7,6},{8,9},{9,8},{10,11... | collective-permute-start | bytes 9437192 | tf_op jit(solution)/shard_map/ppermute | solution.py:643
Sparse Core Ops, SparseCore 0:
  54.5 68.9 all-gather.2

commit v4 on v2

--- a/solution.py
+++ b/solution.py
@@ -265,13 +265,20 @@
         def _():
             pltpu.make_async_copy(extra.at[t - BLOCKS], place(n), sems.at[n]).start()
 
-    load_proj = pltpu.make_async_copy(w_proj, proj, more.at[0])
-    load_gnn = pltpu.make_async_copy(w_gnn, gnn, more.at[1])
+    pieces = 4
+    deep = w_proj.shape[0] // pieces
+    load_proj = [
+        pltpu.make_async_copy(
+            w_proj.at[pl.ds(i * deep, deep), :], proj.at[pl.ds(i * deep, deep), :], more.at[i]
+        )
+        for i in range(pieces)
+    ]
+    load_gnn = pltpu.make_async_copy(w_gnn, gnn, more.at[pieces])
     stores = []
 
     def store(held, out, rows):
         copy = pltpu.make_async_copy(
-            held.at[rows, :], out.at[rows, :], more.at[2 + len(stores)]
+            held.at[rows, :], out.at[rows, :], more.at[pieces + 1 + len(stores)]
         )
         copy.start()
         stores.append(copy)
@@ -279,7 +286,8 @@
     count = BLOCKS * PICKS
     for n in range(count // 2):
         start(n)
-    load_proj.start()
+    for load in load_proj:
+        load.start()
     load_gnn.start()
     for n in range(count // 2, count):
         start(n)
@@ -294,7 +302,8 @@
             texts_v[pl.ds(b * tile, tile), :] = dot(weights, src[b]).astype(bf16)
         store(texts_v, texts, rows)
         if pair == 0:
-            load_proj.wait()
+            for load in load_proj:
+                load.wait()
         summed_v[rows, :] = dot(texts_v[rows, :], proj[...]).astype(bf16)
         store(summed_v, summed, rows)
         if pair == 0:
@@ -329,7 +338,7 @@
             pltpu.VMEM(w_gnn.shape, bf16),
             *[pltpu.VMEM(shape, bf16) for shape in shapes],
             pltpu.SemaphoreType.DMA((BLOCKS * PICKS,)),
-            pltpu.SemaphoreType.DMA((12,)),
+            pltpu.SemaphoreType.DMA((15,)),
         ],
         compiler_params=params(56),
         cost_estimate=cost(2 * slots * depth * width + 2 * adj.size * depth, 22 * 2**20),
@@ -500,16 +509,14 @@
 
 
 def layer_weights_kernel(s0, s1, y0, y1, out):
-    out[...] = (dot_ta(s0[...], y0[...]) + dot_ta(s1[...], y1[...])).astype(bf16)
+    deep = jnp.concatenate([s0[...], s1[...]], axis=0)
+    out[...] = dot_ta(deep, jnp.concatenate([y0[...], y1[...]], axis=0)).astype(bf16)
 
 
 def proj_weights_kernel(x0, x1, t0, t1, y0, y1, g0, g1, before, out):
-    out[...] = (
-        dot_ta(x0[...], y0[...])
-        + dot_ta(x1[...], y1[...])
-        + dot_ta(t0[...], g0[...])
-        + dot_ta(t1[...], g1[...])
-    ).astype(bf16)
+    deep = jnp.concatenate([x0[...], x1[...], t0[...], t1[...]], axis=0)
+    flat = jnp.concatenate([y0[...], y1[...], g0[...], g1[...]], axis=0)
+    out[...] = dot_ta(deep, flat).astype(bf16)
 
 
 def columns_of(array, piece):

time: 317 us -> 317 us (level)
  no operation moved by 1% of the time
where the time goes in v4:
time: 317 us
  blocking collectives  129 us (41%)
  waiting for transfers between devices  101 us (32%)
  Pallas kernels  43.7 us (14%)
  starting transfers between devices  20.8 us (7%)
  between operations  14.3 us (5%)
  local copies, waits for them, and re-layouts  8.22 us (3%)
    all_to_all x2, blocking collectives, between_chips(): return lax.all_to_all(array, CHIPS, split_axis=0, concat_axis=0, tiled=True)  87.4 us
    all_gather x1, waiting for transfers between devices, body(): extra = lax.all_gather(edges[None], MEMBERS, axis=0, tiled=True)  60.3 us
    all_to_all x1, blocking collectives, redistribute(): return lax.all_to_all(buffer, ALL, split_axis=0, concat_axis=0, tiled=True)  41.8 us
    all_to_all x2, waiting for transfers between devices, redistribute(): return lax.all_to_all(buffer, ALL, split_axis=0, concat_axis=0, tiled=True)  35.2 us
    pallas_call x1, Pallas kernels, forward(): pl.pallas_call(forward_kernel, in_specs=[SMEM, ANYWHERE, ANYWHERE, VMEM,...  12.2 us
    all_to_all x2, starting transfers between devices, redistribute(): return lax.all_to_all(buffer, ALL, split_axis=0, concat_axis=0, tiled=True)  11.9 us
    ppermute x7, starting transfers between devices, swap(): return lax.ppermute(array, 'core', [(0, 1), (1, 0)])  8.85 us
    unnamed x30, local copies, waits for them, and re-layouts  7.62 us
  transfers between devices with their start and end apart: 10, of which 5 were waited for; matrix products, arithmetic and copies ran while one was open for 0% of the time, Pallas kernels for 6%

profile of v4, /device:TPU:1, one launch (start us, length us, event | category | flops | bytes accessed | tf_op | source)
XLA Modules:
  0.0 316.9 jit_solution(12072658354946185498)
XLA Ops:
  7.2 0.0 all-gather.3.cloned.1.call-start
  7.2 0.0 copy-start.12
  7.2 3.6 %shard_map.112 = bf16[1024,1024]{1,0:T(8,128)(2,1)} custom-call(bf16[256,2048]{1,0:T(8,128)(2,1)} %t0.1, s32[1,256]{1,0:T(1,128)} %bitcast.29), custom_call_target="tpu_custom_call" | custom-call | flops 1073741824 | bytes 3145728 | tf_op jit(solution)/shard_map/pallas_call | solution.py:151
  10.8 0.0 copy-start.2
  10.8 0.0 copy-start.14
  10.8 41.8 %all_to_all.51 = bf16[128,8,1024]{2,1,0:T(8,128)(2,1)S(1)} all-to-all(bf16[128,8,1024]{2,1,0:T(8,128)(2,1)} %bitcast.23), channel_id=1, replica_groups=mesh['y'=4,'x'=4,'z'=4,'core'=2] {'y','x','z','core'}, dimensions={0} | all-to-all | bytes 4194304 | tf_op jit(solution)/shard_map/all_to_all | solution.py:637
  52.6 0.0 copy-done.12
  52.6 0.9 shard_map.113
  53.5 0.0 copy-start.4
  53.6 0.8 copy-done.4
  54.3 0.0 all-gather.3.cloned.1.call-update
  54.4 0.0 copy-done.2
  54.4 1.3 collective-permute-start
  55.7 0.0 copy-done.14
  55.7 0.6 reshape.33.index
  56.3 0.0 copy-start
  56.3 2.2 copy-done
  58.5 2.0 shard_map.115.embed
  60.5 0.0 copy-start.8
  60.5 1.3 shard_map.114.local
  61.8 0.0 copy-done.8
  61.8 0.0 copy-start.1
  61.8 1.3 copy-done.1
  63.1 0.0 collective-permute-done.t1
  63.1 60.3 %all-gather.3.cloned.1.call-done = bf16[4096,2048]{1,0:T(8,128)(2,1)} async-done(((bf16[128,2048]{1,0:T(8,128)(2,1)}), bf16[4096,2048]{1,0:T(8,128)(2,1)}) %all-gather.3.cloned.1.call-update) | async-done | bytes 16777232 | tf_op jit(solution)/shard_map/all_gather | solution.py:644
  123.5 12.2 %shard_map.116 = (bf16[512,2048]{1,0:T(8,128)(2,1)}, bf16[512,1024]{1,0:T(8,128)(2,1)}, bf16[512,1024]{1,0:T(8,128)(2,1)}, bf16[1024,512]{1,0:T(8,128)(2,1)}) custom-call(s32[1,16]{1,0:T(1,128)} %reshape.33.index, bf16[32,128,2048]{2,1,0:T(8,128)(2,1)} %bitcast.22, bf16[4,128,2048]{2,1,0:T(8,128)(2,1)} %copy-done.1, bf16[4,4,128,128]{3,2,1,0:T(8,128)(2,1)} %bitcast.27, ...), custom_call_target="tpu_custom_call" | custom-call | flops 3221225472 | bytes 23068672 | tf_op jit(solution)/shard_map/pallas_call | solution.py:330
  135.7 7.2 %all-to-all-start.1 = ((bf16[128,8,512]{2,1,0:T(8,128)(2,1)}), bf16[128,8,512]{2,1,0:T(8,128)(2,1)S(1)}, u32[]{:S(2)}, u32[]{:S(2)}) async-start(bf16[128,8,512]{2,1,0:T(8,128)(2,1)} %bitcast.26), calls=%async_computation.1 | async-start | bytes 2097152 | tf_op jit(solution)/shard_map/all_to_all | solution.py:637
  142.9 1.3 collective-permute-start.2
  144.3 17.8 %all-to-all-done.1 = bf16[128,8,512]{2,1,0:T(8,128)(2,1)S(1)} async-done(((bf16[128,8,512]{2,1,0:T(8,128)(2,1)}), bf16[128,8,512]{2,1,0:T(8,128)(2,1)S(1)}, u32[]{:S(2)}, u32[]{:S(2)}) %all-to-all-start.1) | async-done | bytes 1048608 | tf_op jit(solution)/shard_map/all_to_all | solution.py:637
  162.1 0.0 copy-start.13
  162.1 1.0 copy-done.13
  163.1 6.5 %shard_map.117 = (bf16[1024,640]{1,0:T(8,128)(2,1)}, bf16[256,512]{1,0:T(8,128)(2,1)}, bf16[256,512]{1,0:T(8,128)(2,1)}) custom-call(s32[1]{0:T(128)} %bitcast.core.member, bf16[1024,512]{1,0:T(8,128)(2,1)} %bitcast.25, bf16[256,1024]{1,0:T(8,128)(2,1)} %copy-done.8, s32[1,256]{1,0:T(1,128)} %bitcast.30, s32[8,256]{1,0:T(8,128)} %bitcast.28, f32[1,256]{1,0:T(1,128)} %bitcast.31), custom_call_target="tpu_custom_call" | custom-call | flops 8589934592 | bytes 4194304 | tf_op jit(solution)/shard_map/pallas_call | solution.py:439
  169.7 4.6 %all-to-all-start.2 = ((bf16[128,8,640]{2,1,0:T(8,128)(2,1)}), bf16[128,8,640]{2,1,0:T(8,128)(2,1)S(1)}, u32[]{:S(2)}, u32[]{:S(2)}) async-start(bf16[128,8,640]{2,1,0:T(8,128)(2,1)} %bitcast.24), calls=%async_computation.2 | async-start | bytes 2621440 | tf_op jit(solution)/shard_map/all_to_all | solution.py:637
  174.3 1.3 collective-permute-start.4
  175.6 0.1 collective-permute-start.1
  175.7 2.6 collective-permute-done.1.g1
  178.3 0.7 copy-done.10
  179.0 17.3 %all-to-all-done.2 = bf16[128,8,640]{2,1,0:T(8,128)(2,1)S(1)} async-done(((bf16[128,8,640]{2,1,0:T(8,128)(2,1)}), bf16[128,8,640]{2,1,0:T(8,128)(2,1)S(1)}, u32[]{:S(2)}, u32[]{:S(2)}) %all-to-all-start.2) | async-done | bytes 1310752 | tf_op jit(solution)/shard_map/all_to_all | solution.py:637
  196.4 0.0 copy-done.6
  196.4 0.9 shard_map.118
  197.3 1.2 collective-permute-start.5
  198.5 1.6 copy-done.5
  200.1 1.3 shard_map.119
  201.4 0.1 collective-permute-start.3
  201.5 0.0 collective-permute-done.4.s1
  201.5 0.0 collective-permute-done.5.y1
  201.5 0.0 copy-done.7
  201.5 0.0 copy-start.3
  201.5 0.0 copy-start.9
  201.6 0.0 copy-start.11
  201.6 2.7 shard_map.120.before
  204.3 0.0 collective-permute-done.2.x1
  204.3 0.0 collective-permute-done.3.y1
  204.3 0.0 copy-done.3
  204.3 0.0 copy-done.9
  204.4 0.0 copy-done.11
  204.4 5.4 %shard_map.121 = bf16[3072,512]{1,0:T(8,128)(2,1)S(1)} custom-call(bf16[512,2048]{1,0:T(8,128)(2,1)S(1)} %copy-done.3, bf16[512,2048]{1,0:T(8,128)(2,1)} %collective-permute-done.2.x1, bf16[256,2048]{1,0:T(8,128)(2,1)S(1)} %copy-done.2, bf16[256,2048]{1,0:T(8,128)(2,1)} %collective-permute-done.t1, ...), custom_call_target="tpu_custom_call", output_to_operand_aliasing={{}: (8, {})} | custom-call | flops 2147483648 | bytes 10485760 | tf_op jit(solution)/shard_map/pallas_call | solution.py:549
  209.8 44.0 %all_to_all.52.pieces = bf16[64,48,512]{2,1,0:T(8,128)(2,1)S(1)} all-to-all(bf16[64,48,512]{2,1,0:T(8,128)(2,1)S(1)} %bitcast.16), channel_id=1, replica_groups=mesh['y'=4,'x'=4,'z'=4,'core'=2] {'y','x','z'}, dimensions={0} | all-to-all | bytes 6291456 | tf_op jit(solution)/shard_map/all_to_all | solution.py:640
  253.7 1.2 shard_map.122
  255.0 43.5 %all_to_all.53 = bf16[64,48,512]{2,1,0:T(8,128)(2,1)S(1)} all-to-all(bf16[64,48,512]{2,1,0:T(8,128)(2,1)S(1)} %shard_map.122), channel_id=1, replica_groups=mesh['y'=4,'x'=4,'z'=4,'core'=2] {'y','x','z'}, dimensions={0} | all-to-all | bytes 6291456 | tf_op jit(solution)/shard_map/all_to_all | solution.py:640
  298.5 3.5 %collective-permute-start.6 = (bf16[3072,512]{1,0:T(8,128)(2,1)S(1)}, bf16[3072,512]{1,0:T(8,128)(2,1)S(1)}, u32[]{:S(2)}, u32[]{:S(2)}) collective-permute-start(bf16[3072,512]{1,0:T(8,128)(2,1)S(1)} %bitcast.19), channel_id=1, source_target_pairs={{0,1},{1,0},{2,3},{3,2},{4,5},{5,4},{6,7},{7,6},{8,9},{9,8},{10,11... | collective-permute-start | bytes 9437192 | tf_op jit(solution)/shard_map/ppermute | solution.py:634
  301.9 2.8 shard_map.123
  304.7 2.5 collective-permute-done.6.part
  307.2 2.8 shard_map.124
  (4 shorter events, 0.0 us)
Async XLA Ops:
  7.2 116.3 %all-gather.3.cloned.1.call-start = ((), (), s32[]{:S(2)}) async-start(), calls=%async_computation.5 | async-start | bytes 17301504 | tf_op jit(solution)/shard_map/all_gather | solution.py:644
  7.2 45.4 %copy-start.12 = (s32[1,128]{1,0:T(1,128)S(1)}, s32[1,128]{1,0:T(1,128)}, u32[]{:S(2)}) copy-start(s32[1,128]{1,0:T(1,128)} %boundary.1) | copy-start | bytes 1540
  10.8 43.5 %copy-start.2 = (bf16[256,2048]{1,0:T(8,128)(2,1)S(1)}, bf16[256,2048]{1,0:T(8,128)(2,1)}, u32[]{:S(2)}) copy-start(bf16[256,2048]{1,0:T(8,128)(2,1)} %t0.1) | copy-start | bytes 3145732
  10.8 44.9 %copy-start.14 = (s32[1,4,4]{2,1,0:T(4,128)S(1)}, s32[1,4,4]{2,1,0:T(4,128)}, u32[]{:S(2)}) copy-start(s32[1,4,4]{2,1,0:T(4,128)} %param.14) | copy-start | bytes 196
  53.5 0.8 copy-start.4
  54.4 8.8 %collective-permute-start = (bf16[256,2048]{1,0:T(8,128)(2,1)S(1)}, bf16[256,2048]{1,0:T(8,128)(2,1)}, u32[]{:S(2)}, u32[]{:S(2)}) collective-permute-start(bf16[256,2048]{1,0:T(8,128)(2,1)S(1)} %copy-done.2), channel_id=1, source_target_pairs={{0,1},{1,0},{2,3},{3,2},{4,5},{5,4},{6,7},{7,6},{8,9},{9,8},{10,11... | collective-permute-start | bytes 3145736 | tf_op jit(solution)/shard_map/ppermute | solution.py:634
  56.3 2.2 copy-start
  60.5 1.3 copy-start.8
  61.8 1.3 copy-start.1
  135.7 26.4 %all-to-all-start.1 = ((bf16[128,8,512]{2,1,0:T(8,128)(2,1)}), bf16[128,8,512]{2,1,0:T(8,128)(2,1)S(1)}, u32[]{:S(2)}, u32[]{:S(2)}) async-start(bf16[128,8,512]{2,1,0:T(8,128)(2,1)} %bitcast.26), calls=%async_computation.1 | async-start | bytes 2097152 | tf_op jit(solution)/shard_map/all_to_all | solution.py:637
  142.9 61.4 %collective-permute-start.2 = (bf16[512,2048]{1,0:T(8,128)(2,1)}, bf16[512,2048]{1,0:T(8,128)(2,1)}, u32[]{:S(2)}, u32[]{:S(2)}) collective-permute-start(bf16[512,2048]{1,0:T(8,128)(2,1)} %get-tuple-element.35.x0), channel_id=1, source_target_pairs={{0,1},{1,0},{2,3},{3,2},{4,5},{5,4},{6,7},{7,6},{8,9},{9,8},{10,11... | collective-permute-start | bytes 6291464 | tf_op jit(solution)/shard_map/ppermute | solution.py:634
  162.1 1.0 copy-start.13
  163.1 33.3 %copy-start.6 = (bf16[512,1024]{1,0:T(8,128)(2,1)S(1)}, bf16[512,1024]{1,0:T(8,128)(2,1)}, u32[]{:S(2)}) copy-start(bf16[512,1024]{1,0:T(8,128)(2,1)} %get-tuple-element.33.slope_factor) | copy-start | bytes 3145732
  169.7 26.7 %all-to-all-start.2 = ((bf16[128,8,640]{2,1,0:T(8,128)(2,1)}), bf16[128,8,640]{2,1,0:T(8,128)(2,1)S(1)}, u32[]{:S(2)}, u32[]{:S(2)}) async-start(bf16[128,8,640]{2,1,0:T(8,128)(2,1)} %bitcast.24), calls=%async_computation.2 | async-start | bytes 2621440 | tf_op jit(solution)/shard_map/all_to_all | solution.py:637
  174.3 27.2 %collective-permute-start.4 = (bf16[512,1024]{1,0:T(8,128)(2,1)}, bf16[512,1024]{1,0:T(8,128)(2,1)}, u32[]{:S(2)}, u32[]{:S(2)}) collective-permute-start(bf16[512,1024]{1,0:T(8,128)(2,1)} %get-tuple-element.42.s0), channel_id=1, source_target_pairs={{0,1},{1,0},{2,3},{3,2},{4,5},{5,4},{6,7},{7,6},{8,9},{9,8},{10,11... | collective-permute-start | bytes 3145736 | tf_op jit(solution)/shard_map/ppermute | solution.py:634
  175.6 2.7 collective-permute-start.1
  178.3 0.7 copy-start.10
  196.4 5.2 %copy-start.7 = (bf16[512,1024]{1,0:T(8,128)(2,1)S(1)}, bf16[512,1024]{1,0:T(8,128)(2,1)}, u32[]{:S(2)}) copy-start(bf16[512,1024]{1,0:T(8,128)(2,1)} %get-tuple-element.42.s0) | copy-start | bytes 3145732
  197.3 4.2 %collective-permute-start.5 = (bf16[512,512]{1,0:T(8,128)(2,1)S(1)}, bf16[512,512]{1,0:T(8,128)(2,1)S(1)}, u32[]{:S(2)}, u32[]{:S(2)}) collective-permute-start(bf16[512,512]{1,0:T(8,128)(2,1)S(1)} %get-tuple-element.44), channel_id=1, source_target_pairs={{0,1},{1,0},{2,3},{3,2},{4,5},{5,4},{6,7},{7,6},{8,9},{9,8},{10,11... | collective-permute-start | bytes 1572872 | tf_op jit(solution)/shard_map/ppermute | solution.py:634
  198.5 1.6 copy-start.5
  201.4 2.9 collective-permute-start.3
  201.5 2.8 copy-start.3
  201.5 2.8 copy-start.9
  201.6 2.8 copy-start.11
  298.5 8.8 %collective-permute-start.6 = (bf16[3072,512]{1,0:T(8,128)(2,1)S(1)}, bf16[3072,512]{1,0:T(8,128)(2,1)S(1)}, u32[]{:S(2)}, u32[]{:S(2)}) collective-permute-start(bf16[3072,512]{1,0:T(8,128)(2,1)S(1)} %bitcast.19), channel_id=1, source_target_pairs={{0,1},{1,0},{2,3},{3,2},{4,5},{5,4},{6,7},{7,6},{8,9},{9,8},{10,11... | collective-permute-start | bytes 9437192 | tf_op jit(solution)/shard_map/ppermute | solution.py:634
Sparse Core Ops, SparseCore 0:
  54.5 68.9 all-gather.2

commit v5 on v2

--- a/solution.py
+++ b/solution.py
@@ -244,9 +244,35 @@
     )(got)
 
 
+def near_kernel(w_proj, w_gnn, proj, gnn, sems):
+    copies = [
+        pltpu.make_async_copy(w_proj, proj, sems.at[0]),
+        pltpu.make_async_copy(w_gnn, gnn, sems.at[1]),
+    ]
+    for copy in copies:
+        copy.start()
+    for copy in copies:
+        copy.wait()
+
+
+def near(w_proj, w_gnn):
+    return pl.pallas_call(
+        near_kernel,
+        in_specs=[ANYWHERE, ANYWHERE],
+        out_specs=[VMEM, VMEM],
+        out_shape=[
+            jax.ShapeDtypeStruct(w_proj.shape, bf16),
+            jax.ShapeDtypeStruct(w_gnn.shape, bf16),
+        ],
+        scratch_shapes=[pltpu.SemaphoreType.DMA((2,))],
+        compiler_params=params(),
+        cost_estimate=cost(0, 12 * 2**20),
+    )(w_proj, w_gnn)
+
+
 def forward_kernel(
     index, extra, local, adj, w_proj, w_gnn, texts, summed, slope_factor, sent,
-    src, proj, gnn, texts_v, summed_v, slope_v, sent_v, sems, more,
+    src, texts_v, summed_v, slope_v, sent_v, sems, more,
 ):
     tile = extra.shape[1]
     half = sent.shape[1]
@@ -265,24 +291,21 @@
         def _():
             pltpu.make_async_copy(extra.at[t - BLOCKS], place(n), sems.at[n]).start()
 
-    load_proj = pltpu.make_async_copy(w_proj, proj, more.at[0])
-    load_gnn = pltpu.make_async_copy(w_gnn, gnn, more.at[1])
     stores = []
 
     def store(held, out, rows):
         copy = pltpu.make_async_copy(
-            held.at[rows, :], out.at[rows, :], more.at[2 + len(stores)]
+            held.at[rows, :], out.at[rows, :], more.at[len(stores)]
         )
         copy.start()
         stores.append(copy)
 
-    count = BLOCKS * PICKS
-    for n in range(count // 2):
-        start(n)
-    load_proj.start()
-    load_gnn.start()
-    for n in range(count // 2, count):
-        start(n)
+    def start_block(b):
+        for p in range(PICKS):
+            start(b * PICKS + p)
+
+    start_block(0)
+    start_block(1)
     order = weave(tile)
     for pair in range(BLOCKS // 2):
         rows = pl.ds(2 * pair * tile, 2 * tile)
@@ -290,16 +313,14 @@
             for p in range(PICKS):
                 n = b * PICKS + p
                 pltpu.make_async_copy(extra.at[0], place(n), sems.at[n]).wait()
+            if b < 2:
+                start_block(b + 2)
             weights = jnp.concatenate([adj[b, p] for p in range(PICKS)], axis=1)
             texts_v[pl.ds(b * tile, tile), :] = dot(weights, src[b]).astype(bf16)
         store(texts_v, texts, rows)
-        if pair == 0:
-            load_proj.wait()
-        summed_v[rows, :] = dot(texts_v[rows, :], proj[...]).astype(bf16)
+        summed_v[rows, :] = dot(texts_v[rows, :], w_proj[...]).astype(bf16)
         store(summed_v, summed, rows)
-        if pair == 0:
-            load_gnn.wait()
-        before = dot(summed_v[rows, :], gnn[...])
+        before = dot(summed_v[rows, :], w_gnn[...])
         sigma = jax.nn.sigmoid(before)
         out = (before * sigma).astype(bf16)
         slope_v[rows, :] = (sigma * (1.0 + before * (1.0 - sigma))).astype(bf16)
@@ -320,18 +341,16 @@
     shapes = [(slots, depth), (slots, width), (slots, width), (2 * slots, width // 2)]
     return pl.pallas_call(
         forward_kernel,
-        in_specs=[SMEM, ANYWHERE, ANYWHERE, VMEM, ANYWHERE, ANYWHERE],
+        in_specs=[SMEM, ANYWHERE, ANYWHERE, VMEM, VMEM, VMEM],
         out_specs=[ANYWHERE] * 4,
         out_shape=[jax.ShapeDtypeStruct(shape, bf16) for shape in shapes],
         scratch_shapes=[
             pltpu.VMEM((BLOCKS, PICKS * tile, depth), bf16),
-            pltpu.VMEM(w_proj.shape, bf16),
-            pltpu.VMEM(w_gnn.shape, bf16),
             *[pltpu.VMEM(shape, bf16) for shape in shapes],
             pltpu.SemaphoreType.DMA((BLOCKS * PICKS,)),
-            pltpu.SemaphoreType.DMA((12,)),
+            pltpu.SemaphoreType.DMA((10,)),
         ],
-        compiler_params=params(56),
+        compiler_params=params(53),
         cost_estimate=cost(2 * slots * depth * width + 2 * adj.size * depth, 22 * 2**20),
     )(index, extra, local, adj, w_proj, w_gnn)
 
@@ -638,8 +657,13 @@
     local = hold_rows(got)
     embed = embed_rows(text, w_proj)
     other_text = swap(text)
-    extra, local, embed, other_text = together((extra, local, embed, other_text))
-    texts, summed, slope_factor, sent = forward(index, extra, local, adjacency, w_proj, w_gnn)
+    near_proj, near_gnn = near(w_proj, w_gnn)
+    extra, local, embed, other_text, near_proj, near_gnn = together(
+        (extra, local, embed, other_text, near_proj, near_gnn)
+    )
+    texts, summed, slope_factor, sent = forward(
+        index, extra, local, adjacency, near_proj, near_gnn
+    )
     other_texts, other_summed = swap(texts), swap(summed)
     sent, text_keep, text_send = loss_side(
         core, redistribute(sent), embed, t_row, negative_rows, weights

time: 317 us -> 318 us (level)
  local copies, waits for them, and re-layouts: 8.22 us -> 12.3 us
  waiting for transfers between devices: 101 us -> 97.1 us
    unnamed x30 -> x40, local copies, waits for them, and re-layouts: 7.62 us -> 12.2 us
    all_gather x1, waiting for transfers between devices: 60.3 us -> 56.8 us  [body(): extra = lax.all_gather(edges[None], MEMBERS, axis=0, tiled=True)]
where the time goes in v5:
time: 318 us; the launch traced here: 317 us
  blocking collectives  129 us (41%)
  waiting for transfers between devices  97.1 us (31%)
  Pallas kernels  43.8 us (14%)
  starting transfers between devices  20.4 us (6%)
  between operations  14.4 us (5%)
  local copies, waits for them, and re-layouts  12.3 us (4%)
    all_to_all x2, blocking collectives, between_chips(): return lax.all_to_all(array, CHIPS, split_axis=0, concat_axis=0, tiled=True)  87.5 us
    all_gather x1, waiting for transfers between devices, body(): extra = lax.all_gather(edges[None], MEMBERS, axis=0, tiled=True)  56.8 us
    all_to_all x1, blocking collectives, redistribute(): return lax.all_to_all(buffer, ALL, split_axis=0, concat_axis=0, tiled=True)  41.8 us
    all_to_all x2, waiting for transfers between devices, redistribute(): return lax.all_to_all(buffer, ALL, split_axis=0, concat_axis=0, tiled=True)  35.2 us
    unnamed x40, local copies, waits for them, and re-layouts  12.2 us
    pallas_call x1, Pallas kernels, forward(): pl.pallas_call(forward_kernel, in_specs=[SMEM, ANYWHERE, ANYWHERE, VMEM,...  11.8 us
    all_to_all x2, starting transfers between devices, redistribute(): return lax.all_to_all(buffer, ALL, split_axis=0, concat_axis=0, tiled=True)  11.6 us
    ppermute x7, starting transfers between devices, swap(): return lax.ppermute(array, 'core', [(0, 1), (1, 0)])  8.81 us
  transfers between devices with their start and end apart: 10, of which 5 were waited for; matrix products, arithmetic and copies ran while one was open for 0% of the time, Pallas kernels for 6%

profile of v5, /device:TPU:1, one launch (start us, length us, event | category | flops | bytes accessed | tf_op | source)
XLA Modules:
  0.0 317.2 jit_solution(8244534893233048252)
XLA Ops:
  7.2 0.0 all-gather.3.cloned.1.call-start
  7.2 0.0 copy-start.17
  7.2 3.6 %shard_map.112 = bf16[1024,1024]{1,0:T(8,128)(2,1)} custom-call(bf16[256,2048]{1,0:T(8,128)(2,1)} %t0.1, s32[1,256]{1,0:T(1,128)} %bitcast.29), custom_call_target="tpu_custom_call" | custom-call | flops 1073741824 | bytes 3145728 | tf_op jit(solution)/shard_map/pallas_call | solution.py:151
  10.8 0.0 copy-start.3
  10.8 0.0 copy-start.19
  10.8 41.8 %all_to_all.51 = bf16[128,8,1024]{2,1,0:T(8,128)(2,1)S(1)} all-to-all(bf16[128,8,1024]{2,1,0:T(8,128)(2,1)} %bitcast.24), channel_id=1, replica_groups=mesh['y'=4,'x'=4,'z'=4,'core'=2] {'y','x','z','core'}, dimensions={0} | all-to-all | bytes 4194304 | tf_op jit(solution)/shard_map/all_to_all | solution.py:649
  52.6 0.0 copy-done.17
  52.6 0.9 shard_map.113
  53.5 0.0 copy-start.8
  53.6 0.8 copy-done.8
  54.3 0.0 all-gather.3.cloned.1.call-update
  54.4 0.0 copy-done.3
  54.4 1.3 collective-permute-start
  55.7 0.0 copy-done.19
  55.7 0.1 reshape.33.index
  55.8 2.2 copy-done
  58.0 1.6 copy-done.5
  59.6 0.4 shard_map.116
  60.0 2.0 copy-done.1
  62.0 2.0 shard_map.115.embed
  64.1 0.0 copy-start.13
  64.1 1.3 shard_map.114.local
  65.4 0.0 copy-start.2
  65.4 1.3 copy-done.2
  66.7 0.0 collective-permute-done.t1
  66.7 56.8 %all-gather.3.cloned.1.call-done = bf16[4096,2048]{1,0:T(8,128)(2,1)} async-done(((bf16[128,2048]{1,0:T(8,128)(2,1)}), bf16[4096,2048]{1,0:T(8,128)(2,1)}) %all-gather.3.cloned.1.call-update) | async-done | bytes 16777232 | tf_op jit(solution)/shard_map/all_gather | solution.py:656
  123.5 1.0 copy-done.12
  124.5 11.8 %shard_map.117 = (bf16[512,2048]{1,0:T(8,128)(2,1)}, bf16[512,1024]{1,0:T(8,128)(2,1)}, bf16[512,1024]{1,0:T(8,128)(2,1)}, bf16[1024,512]{1,0:T(8,128)(2,1)}) custom-call(s32[1,16]{1,0:T(1,128)S(1)} %reshape.33.index, bf16[32,128,2048]{2,1,0:T(8,128)(2,1)} %bitcast.23, bf16[4,128,2048]{2,1,0:T(8,128)(2,1)} %copy-done.2, ...), custom_call_target="tpu_custom_call" | custom-call | flops 3221225472 | bytes 23068672 | tf_op jit(solution)/shard_map/pallas_call | solution.py:342
  136.3 6.9 %all-to-all-start.1 = ((bf16[128,8,512]{2,1,0:T(8,128)(2,1)}), bf16[128,8,512]{2,1,0:T(8,128)(2,1)S(1)}, u32[]{:S(2)}, u32[]{:S(2)}) async-start(bf16[128,8,512]{2,1,0:T(8,128)(2,1)} %bitcast.26), calls=%async_computation.1 | async-start | bytes 2097152 | tf_op jit(solution)/shard_map/all_to_all | solution.py:649
  143.3 1.3 collective-permute-start.2
  144.6 17.8 %all-to-all-done.1 = bf16[128,8,512]{2,1,0:T(8,128)(2,1)S(1)} async-done(((bf16[128,8,512]{2,1,0:T(8,128)(2,1)}), bf16[128,8,512]{2,1,0:T(8,128)(2,1)S(1)}, u32[]{:S(2)}, u32[]{:S(2)}) %all-to-all-start.1) | async-done | bytes 1048608 | tf_op jit(solution)/shard_map/all_to_all | solution.py:649
  162.4 1.0 copy-done.18
  163.4 6.5 %shard_map.118 = (bf16[1024,640]{1,0:T(8,128)(2,1)}, bf16[256,512]{1,0:T(8,128)(2,1)}, bf16[256,512]{1,0:T(8,128)(2,1)}) custom-call(s32[1]{0:T(128)} %bitcast.core.member, bf16[1024,512]{1,0:T(8,128)(2,1)} %bitcast.27, bf16[256,1024]{1,0:T(8,128)(2,1)} %copy-done.13, s32[1,256]{1,0:T(1,128)} %bitcast.30, s32[8,256]{1,0:T(8,128)} %bitcast.28, f32[1,256]{1,0:T(1,128)} %bitcast.31), custom_call_target="tpu_custom_call" | custom-call | flops 8589934592 | bytes 4194304 | tf_op jit(solution)/shard_map/pallas_call | solution.py:449
  170.0 4.6 %all-to-all-start.2 = ((bf16[128,8,640]{2,1,0:T(8,128)(2,1)}), bf16[128,8,640]{2,1,0:T(8,128)(2,1)S(1)}, u32[]{:S(2)}, u32[]{:S(2)}) async-start(bf16[128,8,640]{2,1,0:T(8,128)(2,1)} %bitcast.25), calls=%async_computation.2 | async-start | bytes 2621440 | tf_op jit(solution)/shard_map/all_to_all | solution.py:649
  174.6 1.3 collective-permute-start.4
  175.9 0.1 collective-permute-start.1
  176.0 2.6 collective-permute-done.1.g1
  178.6 0.7 copy-done.15
  179.3 17.3 %all-to-all-done.2 = bf16[128,8,640]{2,1,0:T(8,128)(2,1)S(1)} async-done(((bf16[128,8,640]{2,1,0:T(8,128)(2,1)}), bf16[128,8,640]{2,1,0:T(8,128)(2,1)S(1)}, u32[]{:S(2)}, u32[]{:S(2)}) %all-to-all-start.2) | async-done | bytes 1310752 | tf_op jit(solution)/shard_map/all_to_all | solution.py:649
  196.7 0.9 shard_map.119
  197.6 1.2 collective-permute-start.5
  198.8 1.6 copy-done.6
  200.4 1.3 shard_map.120
  201.7 0.1 collective-permute-start.3
  201.8 0.0 collective-permute-done.4.s1
  201.8 0.0 collective-permute-done.5.y1
  201.8 0.0 copy-done.11
  201.8 0.0 copy-start.7
  201.8 0.0 copy-start.14
  201.9 0.0 copy-start.16
  201.9 2.7 shard_map.121.before
  204.6 0.0 collective-permute-done.2.x1
  204.6 0.0 collective-permute-done.3.y1
  204.6 0.0 copy-done.7
  204.6 0.0 copy-done.14
  204.7 0.0 copy-done.16
  204.7 5.4 %shard_map.122 = bf16[3072,512]{1,0:T(8,128)(2,1)S(1)} custom-call(bf16[512,2048]{1,0:T(8,128)(2,1)S(1)} %copy-done.7, bf16[512,2048]{1,0:T(8,128)(2,1)} %collective-permute-done.2.x1, bf16[256,2048]{1,0:T(8,128)(2,1)S(1)} %copy-done.3, bf16[256,2048]{1,0:T(8,128)(2,1)} %collective-permute-done.t1, ...), custom_call_target="tpu_custom_call", output_to_operand_aliasing={{}: (8, {})} | custom-call | flops 2147483648 | bytes 10485760 | tf_op jit(solution)/shard_map/pallas_call | solution.py:561
  210.1 44.0 %all_to_all.52.pieces = bf16[64,48,512]{2,1,0:T(8,128)(2,1)S(1)} all-to-all(bf16[64,48,512]{2,1,0:T(8,128)(2,1)S(1)} %bitcast.16), channel_id=1, replica_groups=mesh['y'=4,'x'=4,'z'=4,'core'=2] {'y','x','z'}, dimensions={0} | all-to-all | bytes 6291456 | tf_op jit(solution)/shard_map/all_to_all | solution.py:652
  254.1 1.2 shard_map.123
  255.3 43.5 %all_to_all.53 = bf16[64,48,512]{2,1,0:T(8,128)(2,1)S(1)} all-to-all(bf16[64,48,512]{2,1,0:T(8,128)(2,1)S(1)} %shard_map.123), channel_id=1, replica_groups=mesh['y'=4,'x'=4,'z'=4,'core'=2] {'y','x','z'}, dimensions={0} | all-to-all | bytes 6291456 | tf_op jit(solution)/shard_map/all_to_all | solution.py:652
  298.8 3.4 %collective-permute-start.6 = (bf16[3072,512]{1,0:T(8,128)(2,1)S(1)}, bf16[3072,512]{1,0:T(8,128)(2,1)S(1)}, u32[]{:S(2)}, u32[]{:S(2)}) collective-permute-start(bf16[3072,512]{1,0:T(8,128)(2,1)S(1)} %bitcast.19), channel_id=1, source_target_pairs={{0,1},{1,0},{2,3},{3,2},{4,5},{5,4},{6,7},{7,6},{8,9},{9,8},{10,11... | collective-permute-start | bytes 9437192 | tf_op jit(solution)/shard_map/ppermute | solution.py:646
  302.3 2.8 shard_map.124
  305.1 2.5 collective-permute-done.6.part
  307.5 2.8 shard_map.125
  (15 shorter events, 0.0 us)
Async XLA Ops:
  7.2 116.3 %all-gather.3.cloned.1.call-start = ((), (), s32[]{:S(2)}) async-start(), calls=%async_computation.5 | async-start | bytes 17301504 | tf_op jit(solution)/shard_map/all_gather | solution.py:656
  7.2 45.4 %copy-start.17 = (s32[1,128]{1,0:T(1,128)S(1)}, s32[1,128]{1,0:T(1,128)}, u32[]{:S(2)}) copy-start(s32[1,128]{1,0:T(1,128)} %boundary.1) | copy-start | bytes 1540
  10.8 43.5 %copy-start.3 = (bf16[256,2048]{1,0:T(8,128)(2,1)S(1)}, bf16[256,2048]{1,0:T(8,128)(2,1)}, u32[]{:S(2)}) copy-start(bf16[256,2048]{1,0:T(8,128)(2,1)} %t0.1) | copy-start | bytes 3145732
  10.8 44.9 %copy-start.19 = (s32[1,4,4]{2,1,0:T(4,128)S(1)}, s32[1,4,4]{2,1,0:T(4,128)}, u32[]{:S(2)}) copy-start(s32[1,4,4]{2,1,0:T(4,128)} %param.14) | copy-start | bytes 196
  53.5 0.8 copy-start.8
  54.4 12.3 %collective-permute-start = (bf16[256,2048]{1,0:T(8,128)(2,1)S(1)}, bf16[256,2048]{1,0:T(8,128)(2,1)}, u32[]{:S(2)}, u32[]{:S(2)}) collective-permute-start(bf16[256,2048]{1,0:T(8,128)(2,1)S(1)} %copy-done.3), channel_id=1, source_target_pairs={{0,1},{1,0},{2,3},{3,2},{4,5},{5,4},{6,7},{7,6},{8,9},{9,8},{10,11... | collective-permute-start | bytes 3145736 | tf_op jit(solution)/shard_map/ppermute | solution.py:646
  55.8 2.2 copy-start
  58.0 1.6 copy-start.5
  59.6 2.4 copy-start.1
  62.0 3.3 %copy-start.4 = (bf16[2048,1024]{1,0:T(8,128)(2,1)}, bf16[2048,1024]{1,0:T(8,128)(2,1)S(1)}, u32[]{:S(2)}) copy-start(bf16[2048,1024]{1,0:T(8,128)(2,1)S(1)} %get-tuple-element.34.w_proj) | copy-start | bytes 12582916
  62.0 3.3 %copy-start.9 = (bf16[1024,1024]{1,0:T(8,128)(2,1)}, bf16[1024,1024]{1,0:T(8,128)(2,1)S(1)}, u32[]{:S(2)}) copy-start(bf16[1024,1024]{1,0:T(8,128)(2,1)S(1)} %get-tuple-element.35.w_gnn) | copy-start | bytes 6291460
  64.1 1.3 copy-start.13
  65.4 1.3 copy-start.2
  123.5 1.0 copy-start.12
  136.3 26.1 %all-to-all-start.1 = ((bf16[128,8,512]{2,1,0:T(8,128)(2,1)}), bf16[128,8,512]{2,1,0:T(8,128)(2,1)S(1)}, u32[]{:S(2)}, u32[]{:S(2)}) async-start(bf16[128,8,512]{2,1,0:T(8,128)(2,1)} %bitcast.26), calls=%async_computation.1 | async-start | bytes 2097152 | tf_op jit(solution)/shard_map/all_to_all | solution.py:649
  143.3 61.3 %collective-permute-start.2 = (bf16[512,2048]{1,0:T(8,128)(2,1)}, bf16[512,2048]{1,0:T(8,128)(2,1)}, u32[]{:S(2)}, u32[]{:S(2)}) collective-permute-start(bf16[512,2048]{1,0:T(8,128)(2,1)} %get-tuple-element.43.x0), channel_id=1, source_target_pairs={{0,1},{1,0},{2,3},{3,2},{4,5},{5,4},{6,7},{7,6},{8,9},{9,8},{10,11... | collective-permute-start | bytes 6291464 | tf_op jit(solution)/shard_map/ppermute | solution.py:646
  162.4 1.0 copy-start.18
  163.4 33.3 %copy-start.10 = (bf16[512,1024]{1,0:T(8,128)(2,1)S(1)}, bf16[512,1024]{1,0:T(8,128)(2,1)}, u32[]{:S(2)}) copy-start(bf16[512,1024]{1,0:T(8,128)(2,1)} %get-tuple-element.41.slope_factor) | copy-start | bytes 3145732
  170.0 26.7 %all-to-all-start.2 = ((bf16[128,8,640]{2,1,0:T(8,128)(2,1)}), bf16[128,8,640]{2,1,0:T(8,128)(2,1)S(1)}, u32[]{:S(2)}, u32[]{:S(2)}) async-start(bf16[128,8,640]{2,1,0:T(8,128)(2,1)} %bitcast.25), calls=%async_computation.2 | async-start | bytes 2621440 | tf_op jit(solution)/shard_map/all_to_all | solution.py:649
  174.6 27.2 %collective-permute-start.4 = (bf16[512,1024]{1,0:T(8,128)(2,1)}, bf16[512,1024]{1,0:T(8,128)(2,1)}, u32[]{:S(2)}, u32[]{:S(2)}) collective-permute-start(bf16[512,1024]{1,0:T(8,128)(2,1)} %get-tuple-element.50.s0), channel_id=1, source_target_pairs={{0,1},{1,0},{2,3},{3,2},{4,5},{5,4},{6,7},{7,6},{8,9},{9,8},{10,11... | collective-permute-start | bytes 3145736 | tf_op jit(solution)/shard_map/ppermute | solution.py:646
  175.9 2.7 collective-permute-start.1
  178.6 0.7 copy-start.15
  196.7 5.2 %copy-start.11 = (bf16[512,1024]{1,0:T(8,128)(2,1)S(1)}, bf16[512,1024]{1,0:T(8,128)(2,1)}, u32[]{:S(2)}) copy-start(bf16[512,1024]{1,0:T(8,128)(2,1)} %get-tuple-element.50.s0) | copy-start | bytes 3145732
  197.6 4.2 %collective-permute-start.5 = (bf16[512,512]{1,0:T(8,128)(2,1)S(1)}, bf16[512,512]{1,0:T(8,128)(2,1)S(1)}, u32[]{:S(2)}, u32[]{:S(2)}) collective-permute-start(bf16[512,512]{1,0:T(8,128)(2,1)S(1)} %get-tuple-element.52), channel_id=1, source_target_pairs={{0,1},{1,0},{2,3},{3,2},{4,5},{5,4},{6,7},{7,6},{8,9},{9,8},{10,11... | collective-permute-start | bytes 1572872 | tf_op jit(solution)/shard_map/ppermute | solution.py:646
  198.8 1.6 copy-start.6
  201.7 2.9 collective-permute-start.3
  201.8 2.8 copy-start.7
  201.8 2.8 copy-start.14
  201.9 2.8 copy-start.16
  298.8 8.7 %collective-permute-start.6 = (bf16[3072,512]{1,0:T(8,128)(2,1)S(1)}, bf16[3072,512]{1,0:T(8,128)(2,1)S(1)}, u32[]{:S(2)}, u32[]{:S(2)}) collective-permute-start(bf16[3072,512]{1,0:T(8,128)(2,1)S(1)} %bitcast.19), channel_id=1, source_target_pairs={{0,1},{1,0},{2,3},{3,2},{4,5},{5,4},{6,7},{7,6},{8,9},{9,8},{10,11... | collective-permute-start | bytes 9437192 | tf_op jit(solution)/shard_map/ppermute | solution.py:646
Sparse Core Ops, SparseCore 0:
  54.5 68.9 all-gather.2
